TPU v7x, 128 devices: a whole 4x4x4 slice. The times are simulated.
128 devices in a mesh: lon: 16 (over z_hi, x, core), lat: 8 (over y, z_lo).
Axes of the slice: x: 4, y: 4, z: 4 (z_hi: 2, z_lo: 2; z = z_hi * 2 + z_lo), core: 2. Of those that a mesh axis runs over, the one named last changes fastest.
Arguments:
- tokens: bfloat16 [1024, 256, 512], P('lon', 'lat'), may hold values from -6 to 6
- pad_mask: int32 [1024, 256], replicated, may hold values 0 or 1
- shifts: int32 [2], replicated, may hold values from 1 to 7
- bias_table: float32 [8, 225], replicated, may hold values from -4 to 4
- rel_index: int32 [64, 64], replicated, may hold values from 0 to 224
- w_qkv: bfloat16 [512, 1536], replicated, may hold values from -0.25 to 0.25
- w_out: bfloat16 [512, 512], replicated, may hold values from -0.25 to 0.25
- grad_out: bfloat16 [1024, 256, 512], P('lon', 'lat'), may hold values from -6 to 6
Outputs:
- updated: bfloat16 [1024, 256, 512], P('lon', 'lat')
- tokens_grad: bfloat16 [1024, 256, 512], P('lon', 'lat')
- qkv_weight_grad: float32 [512, 1536], P(('lon', 'lat'))
- out_weight_grad: float32 [512, 512], P(('lon', 'lat'))
All inputs are finite; a program needn't handle non-finite values.
Results may differ from a plain program's by a relative error of at most 0.009.
Values may be sent and summed in bfloat16 or wider, within the bound.
No kernel may reach another device: no remote copies, remote signals or barrier semaphores. Data moves between devices by JAX's collectives and lax.ppermute only.
A program may use at most 128 MiB of HBM per device.

v0:
```python
import jax
import jax.numpy as jnp
from jax import lax
from jax.sharding import PartitionSpec as P

WIN = 8


def from_behind(value, axis, steps):
    count = lax.axis_size(axis)
    pairs = [(source, (source + steps) % count) for source in range(count)]
    return lax.ppermute(value, axis, pairs)


def norm_rows(values):
    floats = values.astype(jnp.float32)
    center = floats - jnp.mean(floats, axis=-1, keepdims=True)
    inv_std = lax.rsqrt(jnp.mean(center * center, axis=-1, keepdims=True) + 1e-05)
    return (center * inv_std, inv_std)


def to_windows(field_in, window):
    span_a, span_b, channels_all = field_in.shape
    blocks = field_in.reshape(span_a // window, window, span_b // window, window, channels_all)
    return blocks.transpose(0, 2, 1, 3, 4).reshape(
        span_a // window, span_b // window, window * window, channels_all
    )


def from_windows(blocks, window):
    count_a, count_b, window_cells, channels_all = blocks.shape
    field_out = blocks.reshape(count_a, count_b, window, window, channels_all).transpose(
        0, 2, 1, 3, 4
    )
    return field_out.reshape(count_a * window, count_b * window, channels_all)


def window_masks(valid_cells, wrapped, window):
    mark_windows = to_windows(jnp.stack([valid_cells, wrapped], axis=-1), window)
    key_valid = mark_windows[..., 0] == 1
    side_marks = mark_windows[..., 1]
    same_side = side_marks[..., :, None] == side_marks[..., None, :]
    diagonal = jnp.eye(window * window, dtype=bool)
    return key_valid[..., None, :] & same_side | diagonal


def bias_lookup(bias_table, rel_index):
    head_count, table_size = bias_table.shape
    window_cells = rel_index.shape[0]
    one_hot = (
        rel_index.reshape(-1)[:, None] == jnp.arange(table_size, dtype=jnp.int32)[None, :]
    ).astype(jnp.float32)
    table_rows = jnp.dot(one_hot, bias_table.T, precision=lax.Precision.HIGHEST)
    return table_rows.reshape(window_cells, window_cells, head_count).transpose(2, 0, 1)


def attend(packed, allowed, position_bias, head_count):
    window_count, window_cells, channels_all = packed.shape
    channels = channels_all // 4
    head_size = channels // head_count
    score_scale = head_size ** (-0.5)
    heads_view = packed.reshape(window_count, window_cells, 4, head_count, head_size)
    queries = heads_view[:, :, 0]
    key_part = heads_view[:, :, 1]
    values = heads_view[:, :, 2]
    attn_grad = heads_view[:, :, 3]
    scores = (
        jnp.einsum("nqhd,nkhd->nhqk", queries, key_part, preferred_element_type=jnp.float32)
        * score_scale
        + position_bias[None]
    )
    unnormed = jnp.where(allowed[:, None], jnp.exp(scores), 0.0)
    normalized = unnormed / jnp.sum(unnormed, axis=-1, keepdims=True)
    normalized_low = normalized.astype(jnp.bfloat16)
    mixed_out = jnp.einsum(
        "nhqk,nkhd->nqhd", normalized_low, values, preferred_element_type=jnp.float32
    ).astype(jnp.bfloat16)
    prob_grad = jnp.einsum("nqhd,nkhd->nhqk", attn_grad, values, preferred_element_type=jnp.float32)
    value_grad = jnp.einsum(
        "nhqk,nqhd->nkhd", normalized_low, attn_grad, preferred_element_type=jnp.float32
    )
    score_grad = normalized * (prob_grad - jnp.sum(normalized * prob_grad, axis=-1, keepdims=True))
    score_low = (score_grad * score_scale).astype(jnp.bfloat16)
    query_grad = jnp.einsum(
        "nhqk,nkhd->nqhd", score_low, key_part, preferred_element_type=jnp.float32
    )
    key_grad = jnp.einsum("nhqk,nqhd->nkhd", score_low, queries, preferred_element_type=jnp.float32)
    window_grads = jnp.stack([query_grad, key_grad, value_grad], axis=2)
    window_grads = window_grads.reshape(window_count, window_cells, 3 * channels).astype(
        jnp.bfloat16
    )
    return (mixed_out.reshape(window_count, window_cells, channels), window_grads)


def project_in(flat_tokens, flat_grad, w_qkv, w_out):
    normed, inv_std = norm_rows(flat_tokens)
    hidden = normed.astype(jnp.bfloat16)
    qkv_rows = jnp.dot(hidden, w_qkv, preferred_element_type=jnp.float32).astype(jnp.bfloat16)
    attn_grad = lax.dot_general(
        flat_grad, w_out, (((1,), (1,)), ((), ())), preferred_element_type=jnp.float32
    ).astype(jnp.bfloat16)
    return (normed, inv_std, hidden, qkv_rows, attn_grad)


def finish(flat_tokens, flat_grad, normed, inv_std, mixed_out, qkv_grad, w_qkv, w_out):
    updated = (
        flat_tokens.astype(jnp.float32)
        + jnp.dot(mixed_out, w_out, preferred_element_type=jnp.float32)
    ).astype(jnp.bfloat16)
    normed_grad = lax.dot_general(
        qkv_grad, w_qkv, (((1,), (1,)), ((), ())), preferred_element_type=jnp.float32
    )
    centred = normed_grad - jnp.mean(normed_grad, axis=-1, keepdims=True)
    centred = centred - normed * jnp.mean(normed_grad * normed, axis=-1, keepdims=True)
    tokens_grad = (flat_grad.astype(jnp.float32) + inv_std * centred).astype(jnp.bfloat16)
    return (updated, tokens_grad)


def local(tokens, pad_mask, shifts, bias_table, rel_index, w_qkv, w_out, grad_out):
    cells_lon, cells_lat, channels = tokens.shape
    head_count = bias_table.shape[0]
    window = WIN
    offset_lon = shifts[0]
    offset_lat = shifts[1]
    zero_index = offset_lon * 0
    total_lon = cells_lon * lax.axis_size("lon")
    total_lat = cells_lat * lax.axis_size("lat")
    place_lon = (
        lax.axis_index("lon") * cells_lon + offset_lon + jnp.arange(cells_lon, dtype=jnp.int32)
    )
    place_lat = (
        lax.axis_index("lat") * cells_lat + offset_lat + jnp.arange(cells_lat, dtype=jnp.int32)
    )
    valid_cells = jnp.take(
        jnp.take(pad_mask, place_lon % total_lon, axis=0), place_lat % total_lat, axis=1
    )
    wrapped = jnp.broadcast_to(
        (place_lat >= total_lat).astype(jnp.int32)[None, :], (cells_lon, cells_lat)
    )
    allowed = window_masks(valid_cells, wrapped, window)
    allowed = allowed.reshape(-1, window * window, window * window)
    position_bias = bias_lookup(bias_table, rel_index)
    flat_tokens = tokens.reshape(-1, channels)
    upstream = grad_out.reshape(-1, channels)
    normed, inv_std, hidden, qkv_rows, attn_grad = project_in(flat_tokens, upstream, w_qkv, w_out)
    packed = jnp.concatenate([qkv_rows, attn_grad], axis=-1).reshape(
        cells_lon, cells_lat, 4 * channels
    )
    arrived = from_behind(packed[:window], "lon", -1)
    extended = jnp.concatenate([packed, arrived], axis=0)
    arrived = from_behind(extended[:, :window], "lat", -1)
    extended = jnp.concatenate([extended, arrived], axis=1)
    framed = lax.dynamic_slice(
        extended, (offset_lon, offset_lat, zero_index), (cells_lon, cells_lat, 4 * channels)
    )
    blocks = to_windows(framed, window)
    count_a, count_b, window_cells, channels_all = blocks.shape
    mixed_part, grad_part = attend(
        blocks.reshape(-1, window_cells, channels_all), allowed, position_bias, head_count
    )
    joined = jnp.concatenate([mixed_part, grad_part], axis=-1)
    result = from_windows(joined.reshape(count_a, count_b, window_cells, 4 * channels), window)
    arrived = from_behind(result[:, cells_lat - window :], "lat", 1)
    joined = jnp.concatenate([arrived, result], axis=1)
    result = lax.dynamic_slice_in_dim(joined, window - offset_lat, cells_lat, 1)
    arrived = from_behind(result[cells_lon - window :], "lon", 1)
    joined = jnp.concatenate([arrived, result], axis=0)
    result = lax.dynamic_slice_in_dim(joined, window - offset_lon, cells_lon, 0).reshape(
        -1, 4 * channels
    )
    mixed_out = result[:, :channels]
    qkv_grad = result[:, channels:]
    updated, tokens_grad = finish(
        flat_tokens, upstream, normed, inv_std, mixed_out, qkv_grad, w_qkv, w_out
    )
    output = updated.reshape(cells_lon, cells_lat, channels)
    output_grad = tokens_grad.reshape(cells_lon, cells_lat, channels)
    qkv_part = lax.dot_general(
        hidden, qkv_grad, (((0,), (0,)), ((), ())), preferred_element_type=jnp.float32
    )
    out_part = lax.dot_general(
        mixed_out, upstream, (((0,), (0,)), ((), ())), preferred_element_type=jnp.float32
    )
    summed = lax.psum_scatter(
        jnp.concatenate([qkv_part, out_part], axis=1),
        ("lon", "lat"),
        scatter_dimension=0,
        tiled=True,
    )
    return (output, output_grad, summed[:, : 3 * channels], summed[:, 3 * channels :])


def solution(mesh):
    in_specs = (P("lon", "lat", None), P(), P(), P(), P(), P(), P(), P("lon", "lat", None))
    out_specs = (
        P("lon", "lat", None),
        P("lon", "lat", None),
        P(("lon", "lat"), None),
        P(("lon", "lat"), None),
    )
    return jax.shard_map(local, mesh=mesh, in_specs=in_specs, out_specs=out_specs, check_vma=False)
```

profile of v0, /device:TPU:0, one launch (start us, length us, event | category | flops | bytes accessed | tf_op | source)
XLA Modules:
  0.0 584.1 jit_solution(13376482818542940963)
XLA Ops:
  14.0 3.7 convolution_convert_fusion
  23.3 5.6 collective-permute-start
  28.9 8.3 %pad_maximum_fusion.1 = bf16[2048,2048]{0,1:T(8,128)(2,1)} fusion(bf16[2048,512]{0,1:T(8,128)(2,1)} %copy-done.7, bf16[2048,1536]{0,1:T(8,128)(2,1)} %copy-done.2), kind=kLoop, calls=%fused_computation.8 | loop fusion | flops 16777216 | bytes 16777216 | tf_op jit(solution)/shard_map/concatenate | solution.py:146
  37.2 12.4 %copy.70 = bf16[2048,2048]{1,0:T(8,128)(2,1)} copy(bf16[2048,2048]{0,1:T(8,128)(2,1)} %pad_maximum_fusion.1) | data formatting | bytes 16777216 | tf_op jit(solution)/shard_map/concatenate | solution.py:146
  53.0 3.9 collective-permute-start.1
  69.6 34.2 %collective-permute-done.1 = bf16[72,8,2048]{2,1,0:T(8,128)(2,1)} collective-permute-done((bf16[72,8,2048]{2,1,0:T(8,128)(2,1)}, bf16[72,8,2048]{2,1,0:T(8,128)(2,1)}, u32[]{:S(2)}, u32[]{:S(2)}) %collective-permute-start.1) | collective-permute-done | bytes 2359328 | tf_op jit(solution)/shard_map/ppermute | solution.py:12
  103.8 15.4 %fusion.4 = bf16[64,32,2048]{2,1,0:T(8,128)(2,1)} fusion(s32[]{:T(128)S(6)} %select_n.101, s32[]{:T(128)S(6)} %select_n.102, bf16[64,32,2048]{2,1,0:T(8,128)(2,1)} %bitcast.115, bf16[8,32,2048]{2,1,0:T(8,128)(2,1)S(1)} %collective-permute-done, bf16[72,8,2048]{2,1,0:T(8,128)(2,1)} %collective-permute-done.1), kind=kLoop, calls=%fused_computation.17 | loop fusion | flops 25165824 | bytes 20185096 | tf_op jit(solution)/shard_map/concatenate | solution.py:152
  119.2 8.3 %copy.72 = bf16[8,4,8,8,2048]{4,3,2,1,0:T(8,128)(2,1)} copy(bf16[8,4,8,8,2048]{4,3,1,2,0:T(8,128)(2,1)} %bitcast.118) | data formatting | bytes 16777216 | tf_op jit(solution)/shard_map/transpose | solution.py:25
  127.4 24.4 %reshape_reshape_reshape.3 = bf16[32,64,4,8,64]{4,3,2,1,0:T(8,128)(2,1)} reshape(bf16[8,4,8,8,2048]{4,3,2,1,0:T(8,128)(2,1)} %copy.72) | data formatting | bytes 16777216 | tf_op jit(solution)/shard_map/reshape;reshape;reshape | solution.py:62
  151.9 12.4 %fusion.71 = (bf16[32,64,1,8,64]{4,3,2,1,0:T(8,128)(2,1)}, bf16[32,64,1,8,64]{4,3,2,1,0:T(8,128)(2,1)}, bf16[32,64,1,8,64]{4,3,2,1,0:T(8,128)(2,1)}, bf16[32,64,1,8,64]{4,3,2,1,0:T(8,128)(2,1)}) fusion(bf16[32,64,4,8,64]{4,3,2,1,0:T(8,128)(2,1)} %reshape_reshape_reshape.3), kind=kLoop, calls=%fused_computation.118 | loop fusion | bytes 16777216 | tf_op jit(solution)/shard_map/slice | solution.py:65
  164.3 6.8 %copy.103 = bf16[32,64,1,8,64]{1,4,3,0,2:T(8,128)(2,1)} copy(bf16[32,64,1,8,64]{4,3,2,1,0:T(8,128)(2,1)} %get-tuple-element.6) | data formatting | bytes 4194304
  171.1 9.2 %fusion.14 = f32[32,8,64,64]{2,3,1,0:T(8,128)} fusion(bf16[32,64,1,8,64]{1,4,3,0,2:T(8,128)(2,1)} %copy.103, bf16[32,64,1,8,64]{4,3,2,1,0:T(8,128)(2,1)} %get-tuple-element.8), kind=kOutput, calls=%fused_computation.34 | convolution fusion | flops 134217728 | bytes 8388608 | tf_op jit(solution)/shard_map/nqhd,nkhd->nhqk/dot_general | solution.py:78
  180.3 6.4 %fusion.7 = (f32[32,8,64]{2,1,0:T(8,128)S(1)}, f32[32,8,64,64]{2,3,1,0:T(8,128)}) fusion(f32[8,64,64]{1,2,0:T(8,128)S(1)} %bitcast.127, pred[32,64,64]{1,2,0:T(8,128)(4,1)S(1)} %and_or_fusion, bf16[32,64,1,8,64]{4,3,2,1,0:T(8,128)(2,1)S(1)} %copy-done.9, bf16[32,64,1,8,64]{4,3,2,1,0:T(8,128)(2,1)S(1)} %copy-done.8), kind=kOutput, calls=%fused_computation.25 | convolution fusion | flops 138395648 | bytes 8716288 | tf_op jit(solution)/shard_map/nqhd,nkhd->nhqk/dot_general | solution.py:68
  186.7 7.8 %convert_bitcast_fusion.3 = bf16[32,64,8,64]{1,3,2,0:T(8,128)(2,1)} fusion(bf16[32,64,1,8,64]{1,4,3,0,2:T(8,128)(2,1)S(1)} %copy-done.3, f32[32,8,64,64]{2,3,1,0:T(8,128)} %get-tuple-element.13, f32[32,8,64]{2,1,0:T(8,128)S(1)} %get-tuple-element.12, f32[8,64,64]{1,2,0:T(8,128)S(1)} %bitcast.128, pred[32,64,64]{1,2,0:T(8,128)(4,1)S(1)} %and_or_fusion), kind=kOutput, calls=%fused_computation.57 | convolution fusion | flops 140509184 | bytes 8716288 | tf_op jit(solution)/shard_map/nhqk,nkhd->nqhd/dot_general | solution.py:75
  194.5 19.2 %convert_bitcast_fusion.2 = bf16[32,64,1,8,64]{1,4,3,0,2:T(8,128)(2,1)} fusion(f32[32,8,64,64]{2,3,1,0:T(8,128)} %fusion.14, bf16[32,64,1,8,64]{4,3,2,1,0:T(8,128)(2,1)} %get-tuple-element.9, f32[32,8,64,64]{2,3,1,0:T(8,128)} %get-tuple-element.13, f32[32,8,64]{2,1,0:T(8,128)S(1)} %get-tuple-element.12, f32[8,64,64]{1,2,0:T(8,128)S(1)} %bitcast.129, ...), kind=kOutput, calls=%fused_computation.56 | convolution fusion | flops 148914240 | bytes 12910592 | tf_op jit(solution)/shard_map/nhqk,nkhd->nqhd/dot_general | solution.py:84
  213.7 19.1 %convert_bitcast_fusion.1 = bf16[32,64,1,8,64]{1,4,3,0,2:T(8,128)(2,1)} fusion(f32[32,8,64,64]{2,3,1,0:T(8,128)} %fusion.14, bf16[32,64,1,8,64]{4,3,2,1,0:T(8,128)(2,1)} %get-tuple-element.7, f32[32,8,64,64]{2,3,1,0:T(8,128)} %get-tuple-element.13, f32[32,8,64]{2,1,0:T(8,128)S(1)} %get-tuple-element.12, f32[8,64,64]{1,2,0:T(8,128)S(1)} %bitcast.130, ...), kind=kOutput, calls=%fused_computation.55 | convolution fusion | flops 148914240 | bytes 12910592 | tf_op jit(solution)/shard_map/nhqk,nqhd->nkhd/dot_general | solution.py:87
  232.7 9.5 %convert_bitcast_fusion = bf16[32,64,1,8,64]{1,4,3,0,2:T(8,128)(2,1)} fusion(bf16[32,64,1,8,64]{4,3,2,1,0:T(8,128)(2,1)} %get-tuple-element.8, f32[32,8,64,64]{2,3,1,0:T(8,128)} %get-tuple-element.13, f32[32,8,64]{2,1,0:T(8,128)S(1)} %get-tuple-element.12, f32[8,64,64]{1,2,0:T(8,128)S(1)} %bitcast.131, pred[32,64,64]{1,2,0:T(8,128)(4,1)S(1)} %and_or_fusion), kind=kOutput, calls=%fused_computation.54 | convolution fusion | flops 140509184 | bytes 8716288 | tf_op jit(solution)/shard_map/nhqk,nqhd->nkhd/dot_general | solution.py:79
  242.2 7.0 %copy.82 = bf16[32,64,8,64]{3,2,1,0:T(8,128)(2,1)} copy(bf16[32,64,8,64]{1,3,2,0:T(8,128)(2,1)} %convert_bitcast_fusion.3) | data formatting | bytes 4194304 | tf_op jit(solution)/shard_map/convert_element_type | solution.py:77
  249.2 6.5 %concatenate.28 = bf16[8,4,8,8,512]{4,3,2,1,0:T(8,128)(2,1)} reshape(bf16[32,64,8,64]{3,2,1,0:T(8,128)(2,1)} %copy.82) | data formatting | bytes 4194304 | tf_op jit(solution)/shard_map/concatenate | solution.py:161
  255.6 11.4 %pad_maximum_fusion = bf16[32,64,3,8,64]{1,4,3,0,2:T(8,128)(2,1)} fusion(bf16[32,64,1,8,64]{1,4,3,0,2:T(8,128)(2,1)} %convert_bitcast_fusion, bf16[32,64,1,8,64]{1,4,3,0,2:T(8,128)(2,1)} %convert_bitcast_fusion.1, bf16[32,64,1,8,64]{1,4,3,0,2:T(8,128)(2,1)} %convert_bitcast_fusion.2), kind=kLoop, calls=%fused_computation.3 | loop fusion | flops 6291456 | bytes 12582912 | tf_op jit(solution)/shard_map/stack | solution.py:88
  267.0 17.2 %copy.91 = bf16[32,64,3,8,64]{4,3,2,1,0:T(8,128)(2,1)} copy(bf16[32,64,3,8,64]{1,4,3,0,2:T(8,128)(2,1)} %pad_maximum_fusion) | data formatting | bytes 12582912 | tf_op jit(solution)/shard_map/stack | solution.py:88
  284.2 16.9 %convert_element_type.62 = bf16[8,4,8,8,1536]{4,3,2,1,0:T(8,128)(2,1)} reshape(bf16[32,64,3,8,64]{4,3,2,1,0:T(8,128)(2,1)} %copy.91) | data formatting | bytes 12582912 | tf_op jit(solution)/shard_map/convert_element_type | solution.py:89
  301.1 8.2 %maximum_bitcast_fusion = bf16[8,8,4,8,2048]{4,3,1,2,0:T(8,128)(2,1)} fusion(bf16[8,4,8,8,1536]{4,3,2,1,0:T(8,128)(2,1)} %convert_element_type.62, bf16[8,4,8,8,512]{4,3,2,1,0:T(8,128)(2,1)} %concatenate.28), kind=kLoop, calls=%fused_computation.18 | loop fusion | flops 16777216 | bytes 16777216 | tf_op jit(solution)/shard_map/transpose | solution.py:32
  309.3 8.3 %copy.92 = bf16[8,8,4,8,2048]{4,3,2,1,0:T(8,128)(2,1)} copy(bf16[8,8,4,8,2048]{4,3,1,2,0:T(8,128)(2,1)} %maximum_bitcast_fusion) | data formatting | bytes 16777216 | tf_op jit(solution)/shard_map/transpose | solution.py:32
  322.9 43.5 %collective-permute-done.2 = bf16[64,8,2048]{2,1,0:T(8,128)(2,1)} collective-permute-done((bf16[64,8,2048]{2,1,0:T(8,128)(2,1)}, bf16[64,8,2048]{2,1,0:T(8,128)(2,1)}, u32[]{:S(2)}, u32[]{:S(2)}) %collective-permute-start.2) | collective-permute-done | bytes 2097184 | tf_op jit(solution)/shard_map/ppermute | solution.py:12
  366.4 12.9 %fusion.2 = bf16[64,32,2048]{2,1,0:T(8,128)(2,1)} fusion(s32[]{:T(128)S(6)} %select_n.114, bf16[64,8,2048]{2,1,0:T(8,128)(2,1)} %collective-permute-done.2, bf16[64,32,2048]{2,1,0:T(8,128)(2,1)} %bitcast.117), kind=kLoop, calls=%fused_computation.15 | loop fusion | flops 16777216 | bytes 18874372 | tf_op jit(solution)/shard_map/concatenate | solution.py:164
  383.0 20.0 %collective-permute-done.3 = bf16[8,32,2048]{2,1,0:T(8,128)(2,1)S(1)} collective-permute-done((bf16[8,32,2048]{2,1,0:T(8,128)(2,1)}, bf16[8,32,2048]{2,1,0:T(8,128)(2,1)S(1)}, u32[]{:S(2)}, u32[]{:S(2)}) %collective-permute-start.3) | collective-permute-done | bytes 1048608 | tf_op jit(solution)/shard_map/ppermute | solution.py:12
  402.9 7.6 %fusion.1 = bf16[64,32,2048]{2,1,0:T(8,128)(2,1)} fusion(s32[]{:T(128)S(6)} %select_n.115, bf16[8,32,2048]{2,1,0:T(8,128)(2,1)S(1)} %collective-permute-done.3, bf16[64,32,2048]{2,1,0:T(8,128)(2,1)} %fusion.2), kind=kLoop, calls=%fused_computation.14 | loop fusion | flops 4194304 | bytes 17825796 | tf_op jit(solution)/shard_map/concatenate | solution.py:167
  410.5 6.6 %fusion.8 = f32[512,1536]{1,0:T(8,128)S(1)} fusion(bf16[2048,512]{1,0:T(8,128)(2,1)} %copy-done.10, bf16[2048,2048]{1,0:T(8,128)(2,1)} %bitcast.119), kind=kOutput, calls=%fused_computation.26 | convolution fusion | flops 3221225472 | bytes 11534336 | tf_op jit(solution)/shard_map/dot_general | solution.py:178
  422.3 7.1 %fusion.70 = (f32[2048]{0:T(1024)S(1)}, f32[2048]{0:T(1024)S(1)}, f32[2048,512]{1,0:T(8,128)S(1)}) fusion(f32[2048]{0:T(1024)S(1)} %copy-done.14, f32[2048]{0:T(1024)S(1)} %copy-done.12, bf16[64,32,512]{2,1,0:T(8,128)(2,1)} %param.8, bf16[512,1536]{1,0:T(8,128)(2,1)S(1)} %copy-done, bf16[2048,2048]{1,0:T(8,128)(2,1)} %bitcast.121), kind=kOutput, calls=%fused_computation.117 | convolution fusion | flops 3227512832 | bytes 14188544 | tf_op jit(solution)/shard_map/dot_general | solution.py:110
  429.5 4.4 fusion.29
  436.6 137.4 %all-reduce.3.cloned.1.call-done = f32[512,2048]{1,0:T(8,128)} async-done(((f32[512,2048]{1,0:T(8,128)}), f32[512,2048]{1,0:T(8,128)}) %all-reduce.3.cloned.1.call-update) | async-done | bytes 4194320
  (92 shorter events, 40.0 us)
Async XLA Ops:
  7.2 6.8 %copy-start = (bf16[512,1536]{1,0:T(8,128)(2,1)S(1)}, bf16[512,1536]{1,0:T(8,128)(2,1)}, u32[]{:S(2)}) copy-start(bf16[512,1536]{1,0:T(8,128)(2,1)} %param.13) | copy-start | bytes 4718596
  7.2 566.8 %all-reduce.3.cloned.1.call-start = ((), (), s32[]{:S(2)}) async-start(), calls=%async_computation | async-start | bytes 8388608
  11.9 5.8 copy-start.11
  12.0 5.7 copy-start.13
  14.0 3.8 copy-start.10
  14.0 3.8 copy-start.4
  14.0 3.8 copy-start.17
  17.7 2.7 copy-start.2
  20.4 1.3 copy-start.7
  23.3 26.3 %collective-permute-start = (bf16[8,32,2048]{2,1,0:T(8,128)(2,1)}, bf16[8,32,2048]{2,1,0:T(8,128)(2,1)S(1)}, u32[]{:S(2)}, u32[]{:S(2)}) collective-permute-start(bf16[8,32,2048]{2,1,0:T(8,128)(2,1)} %bitcast.126), channel_id=1, source_target_pairs={{0,120},{8,0},{16,8},{24,16},{32,24},{40,32},{48,40},{56,48},{64,5... | collective-permute-start | bytes 3145736 | tf_op jit(solution)/shard_map/ppermute | solution.py:12
  49.6 7.3 %copy-start.16 = (s32[2]{0:T(128)S(1)}, s32[2]{0:T(128)}, u32[]{:S(2)}) copy-start(s32[2]{0:T(128)} %param.10) | copy-start | bytes 28
  49.6 15.0 %copy-start.15 = (s32[64,64]{1,0:T(8,128)S(1)}, s32[64,64]{1,0:T(8,128)}, u32[]{:S(2)}) copy-start(s32[64,64]{1,0:T(8,128)} %param.12) | copy-start | bytes 49156
  49.6 15.1 %copy-start.19 = (f32[8,225]{1,0:T(8,128)S(1)}, f32[8,225]{1,0:T(8,128)}, u32[]{:S(2)}) copy-start(f32[8,225]{1,0:T(8,128)} %param.11) | copy-start | bytes 21604
  53.0 50.8 %collective-permute-start.1 = (bf16[72,8,2048]{2,1,0:T(8,128)(2,1)}, bf16[72,8,2048]{2,1,0:T(8,128)(2,1)}, u32[]{:S(2)}, u32[]{:S(2)}) collective-permute-start(bf16[72,8,2048]{2,1,0:T(8,128)(2,1)} %pad_maximum_fusion.3), channel_id=1, source_target_pairs={{0,7},{1,0},{2,1},{3,2},{4,3},{5,4},{6,5},{7,6},{8,15},{9,8},{10,9... | collective-permute-start | bytes 7077896 | tf_op jit(solution)/shard_map/ppermute | solution.py:12
  171.1 9.2 %copy-start.8 = (bf16[32,64,1,8,64]{4,3,2,1,0:T(8,128)(2,1)S(1)}, bf16[32,64,1,8,64]{4,3,2,1,0:T(8,128)(2,1)}, u32[]{:S(2)}) copy-start(bf16[32,64,1,8,64]{4,3,2,1,0:T(8,128)(2,1)} %get-tuple-element.7) | copy-start | bytes 6291460
  171.1 9.2 %copy-start.9 = (bf16[32,64,1,8,64]{4,3,2,1,0:T(8,128)(2,1)S(1)}, bf16[32,64,1,8,64]{4,3,2,1,0:T(8,128)(2,1)}, u32[]{:S(2)}) copy-start(bf16[32,64,1,8,64]{4,3,2,1,0:T(8,128)(2,1)} %get-tuple-element.9) | copy-start | bytes 6291460
  180.3 6.4 %copy-start.3 = (bf16[32,64,1,8,64]{1,4,3,0,2:T(8,128)(2,1)S(1)}, bf16[32,64,1,8,64]{1,4,3,0,2:T(8,128)(2,1)}, u32[]{:S(2)}) copy-start(bf16[32,64,1,8,64]{1,4,3,0,2:T(8,128)(2,1)} %copy.103) | copy-start | bytes 6291460
  320.7 45.7 %collective-permute-start.2 = (bf16[64,8,2048]{2,1,0:T(8,128)(2,1)}, bf16[64,8,2048]{2,1,0:T(8,128)(2,1)}, u32[]{:S(2)}, u32[]{:S(2)}) collective-permute-start(bf16[64,8,2048]{2,1,0:T(8,128)(2,1)} %slice.80), channel_id=1, source_target_pairs={{0,1},{1,2},{2,3},{3,4},{4,5},{5,6},{6,7},{7,0},{8,9},{9,10},{10,1... | collective-permute-start | bytes 6291464 | tf_op jit(solution)/shard_map/ppermute | solution.py:12
  381.6 21.3 %collective-permute-start.3 = (bf16[8,32,2048]{2,1,0:T(8,128)(2,1)}, bf16[8,32,2048]{2,1,0:T(8,128)(2,1)S(1)}, u32[]{:S(2)}, u32[]{:S(2)}) collective-permute-start(bf16[8,32,2048]{2,1,0:T(8,128)(2,1)} %slice.81), channel_id=1, source_target_pairs={{0,8},{8,16},{16,24},{24,32},{32,40},{40,48},{48,56},{56,64},{64,7... | collective-permute-start | bytes 3145736 | tf_op jit(solution)/shard_map/ppermute | solution.py:12
  410.5 6.7 %copy-start.5 = (bf16[64,32,512]{2,1,0:T(8,128)(2,1)S(1)}, bf16[64,32,512]{2,1,0:T(8,128)(2,1)}, u32[]{:S(2)}) copy-start(bf16[64,32,512]{2,1,0:T(8,128)(2,1)} %param.15) | copy-start | bytes 6291460
  420.0 2.3 copy-start.12
  420.0 2.3 copy-start.14
  422.3 7.1 %copy-start.1 = (bf16[64,32,512]{2,1,0:T(8,128)(2,1)S(1)}, bf16[64,32,512]{2,1,0:T(8,128)(2,1)}, u32[]{:S(2)}) copy-start(bf16[64,32,512]{2,1,0:T(8,128)(2,1)} %param.8) | copy-start | bytes 6291460
  422.3 7.1 %copy-start.18 = (bf16[512,512]{1,0:T(8,128)(2,1)S(1)}, bf16[512,512]{1,0:T(8,128)(2,1)}, u32[]{:S(2)}) copy-start(bf16[512,512]{1,0:T(8,128)(2,1)} %param.14) | copy-start | bytes 1572868
  429.4 4.5 copy-start.6
Sparse Core Ops, SparseCore 0:
  422.4 151.5 all-reduce.2
where the time goes:
time: 593 us; the launch traced here: 584 us
  waiting for transfers between devices  235 us (40%)
  local copies, waits for them, and re-layouts  137 us (23%)
  matrix products  99.6 us (17%)
  other arithmetic  79.7 us (13%)
  between operations  22.8 us (4%)
  starting transfers between devices  10.5 us (2%)
    unnamed x2, waiting for transfers between devices  137 us
    ppermute x4, waiting for transfers between devices, from_behind(): return lax.ppermute(value, axis, pairs)  97.6 us
    another operation x1, local copies, waits for them, and re-layouts, attend(): packed.reshape(window_count, window_cells, 4, head_count, head_size)  24.4 us
    dot_general x1, matrix products, attend(): jnp.einsum('nhqk,nkhd->nqhd', score_low, key_part, preferred_element_type...  19.2 us
    dot_general x1, matrix products, attend(): jnp.einsum('nhqk,nqhd->nkhd', score_low, queries, preferred_element_type=...  19.1 us
    another operation x1, local copies, waits for them, and re-layouts, attend(): window_grads = jnp.stack([query_grad, key_grad, value_grad], axis=2)  17.2 us
    convert_element_type x1, local copies, waits for them, and re-layouts, attend(): window_grads.reshape(window_count, window_cells, 3 * channels)  16.9 us
    concatenate x1, other arithmetic, local(): extended = jnp.concatenate([extended, arrived], axis=1)  15.4 us
  transfers between devices with their start and end apart: 5, of which 4 were waited for; matrix products, arithmetic and copies ran while one was open for 7% of the time, Pallas kernels for 0%

commit v1 on v0

v1 whole, which is shorter than its diff:
```python
import jax
import jax.numpy as jnp
from jax import lax
from jax.experimental import pallas as pl
from jax.experimental.pallas import tpu as pltpu
from jax.sharding import Mesh, PartitionSpec as P

WIN = 8
CELLS = 64
D = 512
HEADS = 8
GROUP = 256
BF = jnp.bfloat16
F32 = jnp.float32
LOG2E = 1.4426950408889634
SCALE = 0.125
VMEM_LIMIT = 56 * 2**20


def dot_nn(a, b):
    return lax.dot_general(a, b, (((1,), (0,)), ((), ())), preferred_element_type=F32)


def dot_nt(a, b):
    return lax.dot_general(a, b, (((1,), (1,)), ((), ())), preferred_element_type=F32)


def dot_tn(a, b):
    return lax.dot_general(a, b, (((0,), (0,)), ((), ())), preferred_element_type=F32)


def iota(shape, dim):
    return lax.broadcasted_iota(jnp.int32, shape, dim)


def load_window(tok, grad, i, j, row, xg, hid, istd):
    x = tok[pl.ds(i, WIN), pl.ds(j, WIN), :].reshape(CELLS, D)
    center = x - jnp.mean(x, axis=-1, keepdims=True)
    inv = lax.rsqrt(jnp.mean(center * center, axis=-1, keepdims=True) + 1e-05)
    hid[pl.ds(row, CELLS), :] = (center * inv).astype(BF)
    istd[pl.ds(row, CELLS), :] = jnp.broadcast_to(inv, (CELLS, 128))
    xg[pl.ds(row, CELLS), :] = grad[pl.ds(i, WIN), pl.ds(j, WIN), :].reshape(CELLS, D).astype(BF)


def project(rows, chunk, hid, xg, w_qkv, w_out, qkvg):
    def step(c, carry):
        at = pl.ds(pl.multiple_of(c * chunk, 64), chunk)
        qkvg[at, : 3 * D] = dot_nn(hid[at, :], w_qkv[...]).astype(BF)
        qkvg[at, 3 * D :] = dot_nt(xg[at, :], w_out[...]).astype(BF)
        return carry

    lax.fori_loop(0, rows // chunk, step, 0)


def attend(first, count, thr_of, keys, bias, qkvg, mix, dq):
    lane = iota((CELLS, 128), 1)
    cell = iota((CELLS, 128), 0)
    diag = (lane & 63) == cell
    block = (iota((GROUP, GROUP), 0) >> 6) == (iota((GROUP, GROUP), 1) >> 6)
    ones = jnp.where(block, 1.0, 0.0).astype(BF)
    zero = jnp.zeros((GROUP, GROUP), BF)
    low_half = lane < 64
    units = []
    for w in range(count):
        row = pl.multiple_of((first + w) * CELLS, CELLS)
        thr = thr_of(w)
        same = ((lane & 7) >= thr) == ((cell & 7) >= thr)
        valid = jnp.broadcast_to(keys[pl.ds(first + w, 1), :], (CELLS, 128)) > 0
        ok = (valid & same) | diag
        ok = jnp.concatenate([ok, ok], axis=1)
        for h in range(2):
            c = h * GROUP
            at = pl.ds(row, CELLS)
            q = qkvg[at, c : c + GROUP]
            k = qkvg[at, D + c : D + c + GROUP]
            v = qkvg[at, 2 * D + c : 2 * D + c + GROUP]
            g = qkvg[at, 3 * D + c : 3 * D + c + GROUP]
            kbd = jnp.where(block, jnp.concatenate([k] * 4, axis=0), zero)
            vbd = jnp.where(block, jnp.concatenate([v] * 4, axis=0), zero)
            s = dot_nt(q, kbd)
            pg = dot_nt(g, vbd)
            e = jnp.where(ok, jnp.exp2(s * (SCALE * LOG2E) + bias[:, c : c + GROUP]), 0.0)
            units.append((at, c, q, g, kbd, vbd, e, pg))
    total = dot_nn(jnp.concatenate([u[6].astype(BF) for u in units], axis=0), ones)
    probs = []
    for n, u in enumerate(units):
        probs.append(u[6] / total[n * CELLS : (n + 1) * CELLS])
    dots = dot_nn(
        jnp.concatenate([(p * u[7]).astype(BF) for p, u in zip(probs, units)], axis=0), ones
    )
    for n, (at, c, q, g, kbd, vbd, e, pg) in enumerate(units):
        p = probs[n]
        p_low = p.astype(BF)
        ds = (p * (pg - dots[n * CELLS : (n + 1) * CELLS]) * SCALE).astype(BF)
        mix[at, c : c + GROUP] = dot_nn(p_low, vbd).astype(BF)
        dq[at, c : c + GROUP] = dot_nn(ds, kbd).astype(BF)
        for t in range(2):
            lo, hi = t * 128, t * 128 + 128
            kg = dot_tn(ds[:, lo:hi], q[:, lo:hi])
            vg = dot_tn(p_low[:, lo:hi], g[:, lo:hi])
            dq[at, D + c + lo : D + c + hi] = jnp.where(low_half, kg[:64], kg[64:]).astype(BF)
            dq[at, 2 * D + c + lo : 2 * D + c + hi] = jnp.where(low_half, vg[:64], vg[64:]).astype(BF)


def finish_window(tok, grad, i, j, update, normed_grad, hidden, inv):
    at = (pl.ds(i, WIN), pl.ds(j, WIN), slice(None))
    tok[at] = tok[at] + update.reshape(WIN, WIN, D)
    normed = hidden.astype(F32)
    centred = normed_grad - jnp.mean(normed_grad, axis=-1, keepdims=True)
    centred = centred - normed * jnp.mean(normed_grad * normed, axis=-1, keepdims=True)
    grad[at] = grad[at] + (inv * centred).reshape(WIN, WIN, D)


def interior_kernel(
    sc, tokens, grads, keys, bias, w_qkv, w_out,
    updated, tokens_grad, w_part,
    tok, grad, xg, hid, istd, qkvg, mix, dq,
):
    s0, s1 = sc[0], sc[1]

    def fill(n, carry):
        at = pl.ds(n * 4, 4)
        for ref, src in ((tok, tokens), (grad, grads)):
            ref[at, :, :] = pltpu.roll(src[at, :, :].astype(F32), 32 - s1, 1)
        return carry

    lax.fori_loop(0, 16, fill, 0)

    def load(a, carry):
        for b in range(3):
            row = pl.multiple_of((a * 3 + b) * CELLS, CELLS)
            load_window(tok, grad, s0 + a * WIN, b * WIN, row, xg, hid, istd)
        return carry

    lax.fori_loop(0, 7, load, 0)
    project(21 * CELLS, 448, hid, xg, w_qkv, w_out, qkvg)

    def windows(a, carry):
        attend(a * 3, 3, lambda w: 8, keys, bias, qkvg, mix, dq)
        return carry

    lax.fori_loop(0, 7, windows, 0)

    def finish(a, carry):
        at = pl.ds(pl.multiple_of(a * 192, 64), 192)
        update = dot_nn(mix[at, :], w_out[...])
        normed_grad = dot_nt(dq[at, :], w_qkv[...])
        hidden = hid[at, :]
        inv = istd[at, :]
        for b in range(3):
            r = slice(b * CELLS, (b + 1) * CELLS)
            finish_window(
                tok, grad, s0 + a * WIN, b * WIN,
                update[r], normed_grad[r], hidden[r], inv[r, :1],
            )
        return carry

    lax.fori_loop(0, 7, finish, 0)
    for b in range(2):
        r = slice(b * 256, (b + 1) * 256)
        w_part[r, : 3 * D] = dot_tn(hid[:, r], dq[...])
        w_part[r, 3 * D :] = dot_tn(mix[:, r], xg[...])

    def store(n, carry):
        at = pl.ds(n * 4, 4)
        for ref, out in ((tok, updated), (grad, tokens_grad)):
            out[at, :, :] = pltpu.roll(ref[at, :, :], s1, 1).astype(BF)
        return carry

    lax.fori_loop(0, 16, store, 0)


def edge_kernel(
    sc, tokens, grads, halo_lon, halo_lat, halo_cor, keys, bias, w_qkv, w_out, w_first,
    edge_lat, edge_lon, out_lat, out_lon, out_cor, w_mine, w_other,
    tok, grad, xg, hid, istd, qkvg, mix, dq, w_sum,
):
    s0, s1, core, thr_edge = sc[0], sc[1], sc[2], sc[3]

    def fill(n, carry):
        at = pl.ds(n * 8, 8)
        for ref, src, c in ((tok, tokens, 0), (grad, grads, D)):
            rows = [src[at, 24:32, :].astype(F32), halo_lat[at, :, c : c + D].astype(F32)]
            ref[at, 24:32, :] = pltpu.roll(jnp.concatenate(rows, axis=1), 16 - s1, 1)[:, :8]
        return carry

    lax.fori_loop(0, 7, fill, 0)
    for r in range(0, 8, 4):
        for ref, src, c in ((tok, tokens, 0), (grad, grads, D)):
            rows = [src[56 + r : 60 + r], halo_lat[56 + r : 60 + r, :, c : c + D]]
            rows = jnp.concatenate([part.astype(F32) for part in rows], axis=1)
            ref[56 + r : 60 + r] = pltpu.roll(rows, 40 - s1, 1)[:, :32]
            rows = [halo_lon[r : r + 4, :, c : c + D], halo_cor[r : r + 4, :, c : c + D]]
            rows = jnp.concatenate([part.astype(F32) for part in rows], axis=1)
            ref[64 + r : 68 + r] = pltpu.roll(rows, 40 - s1, 1)[:, :32]

    def load_side(a, carry):
        row = pl.multiple_of(a * CELLS, CELLS)
        load_window(tok, grad, s0 + a * WIN, 24, row, xg, hid, istd)
        return carry

    lax.fori_loop(0, 7, load_side, 0)
    for b in range(4):
        load_window(tok, grad, s0 + 56, b * WIN, (7 + b) * CELLS, xg, hid, istd)
    tail = slice(11 * CELLS, 12 * CELLS)
    xg[tail, :] = jnp.zeros((CELLS, D), BF)
    hid[tail, :] = jnp.zeros((CELLS, D), BF)
    istd[tail, :] = jnp.zeros((CELLS, 128), F32)
    project(12 * CELLS, 384, hid, xg, w_qkv, w_out, qkvg)

    def windows(a, carry):
        def thr_of(w):
            n = a * 3 + w
            return jnp.where((n < 7) | (n == 10), thr_edge, 8)

        attend(a * 3, 3, thr_of, keys, bias, qkvg, mix, dq)
        return carry

    lax.fori_loop(0, 4, windows, 0)
    for b in range(2):
        r = slice(b * 256, (b + 1) * 256)
        w_sum[r, : 3 * D] = w_first[r, : 3 * D] + dot_tn(hid[:, r], dq[...])
        w_sum[r, 3 * D :] = w_first[r, 3 * D :] + dot_tn(mix[:, r], xg[...])

    def split(n, carry):
        to = pl.ds(pl.multiple_of(n * 32, 32), 32)
        w_mine[to, :] = w_sum[pl.ds(pl.multiple_of((2 * n + core) * 32, 32), 32), :].astype(BF)
        w_other[to, :] = w_sum[pl.ds(pl.multiple_of((2 * n + 1 - core) * 32, 32), 32), :].astype(BF)
        return carry

    lax.fori_loop(0, 8, split, 0)

    for base, count in ((0, 4), (4, 4), (8, 3)):
        at = slice(base * CELLS, (base + count) * CELLS)
        update = dot_nn(mix[at, :], w_out[...])
        normed_grad = dot_nt(dq[at, :], w_qkv[...])
        for b in range(count):
            r = slice(b * CELLS, (b + 1) * CELLS)
            rr = slice((base + b) * CELLS, (base + b + 1) * CELLS)
            n = base + b
            a, c = (n, 3) if n < 7 else (7, n - 7)
            finish_window(
                tok, grad, s0 + a * WIN, c * WIN,
                update[r], normed_grad[r], hid[rr, :], istd[rr, :1],
            )

    def store(n, carry):
        at = pl.ds(n * 8, 8)
        for ref, c in ((tok, 0), (grad, D)):
            rows = ref[at, 24:32, :]
            rows = jnp.concatenate([rows, jnp.zeros_like(rows)], axis=1)
            rows = pltpu.roll(rows, s1, 1).astype(BF)
            edge_lat[at, :, c : c + D] = rows[:, :8]
            out_lat[at, :, c : c + D] = rows[:, 8:]
        return carry

    lax.fori_loop(0, 7, store, 0)
    for r in range(0, 8, 4):
        for ref, c in ((tok, 0), (grad, D)):
            cols = slice(c, c + D)
            pad = jnp.zeros((4, 8, D), F32)
            rows = pltpu.roll(jnp.concatenate([ref[56 + r : 60 + r], pad], axis=1), s1, 1)
            rows = rows.astype(BF)
            edge_lon[r : r + 4, :, cols] = rows[:, :32]
            edge_lat[56 + r : 60 + r, :, cols] = rows[:, 24:32]
            out_lat[56 + r : 60 + r, :, cols] = rows[:, 32:]
            rows = pltpu.roll(jnp.concatenate([ref[64 + r : 68 + r], pad], axis=1), s1, 1)
            rows = rows.astype(BF)
            out_lon[r : r + 4, :, cols] = rows[:, :32]
            out_cor[r : r + 4, :, cols] = rows[:, 32:]


def merge_kernel(
    sc, updated, tokens_grad, edge_lat, edge_lon, in_lat, in_lon, in_cor, out_updated, out_grad
):
    s0, s1 = sc[0], sc[1]
    for src, out, c in ((updated, out_updated, 0), (tokens_grad, out_grad, D)):
        cols = slice(c, c + D)
        out[:, 8:24, :] = src[:, 8:24, :]
        lat = iota((64, 8, D), 1)
        lon = iota((64, 8, D), 0)
        left = jnp.where(lat < s1, in_lat[:, :, cols].astype(F32), src[:, 0:8, :].astype(F32))
        out[:, 0:8, :] = left.astype(BF)
        right = jnp.where(lat >= s1, edge_lat[:, :, cols].astype(F32), src[:, 24:32, :].astype(F32))
        out[:, 24:32, :] = right.astype(BF)
        lat = iota((8, 32, D), 1)
        lon = iota((8, 32, D), 0)
        low = out[56:64, :, :].astype(F32)
        low = jnp.where((lon >= s0) & (lat >= s1), edge_lon[:, :, cols].astype(F32), low)
        out[56:64, :, :] = low.astype(BF)
        top = out[0:8, :, :].astype(F32)
        top = jnp.where((lon < s0) & (lat >= s1), in_lon[:, :, cols].astype(F32), top)
        out[0:8, :, :] = top.astype(BF)
        lat = iota((8, 8, D), 1)
        lon = iota((8, 8, D), 0)
        spot = out[0:8, 0:8, :].astype(F32)
        spot = jnp.where((lon < s0) & (lat < s1), in_cor[:, :, cols].astype(F32), spot)
        out[0:8, 0:8, :] = spot.astype(BF)


def vmem(shape, dtype):
    return pltpu.VMEM(shape, dtype)


def sds(shape, dtype):
    return jax.ShapeDtypeStruct(shape, dtype)


def call(kernel, out_shape, scratch, count):
    in_specs = [pl.BlockSpec(memory_space=pltpu.SMEM)]
    in_specs += [pl.BlockSpec(memory_space=pltpu.VMEM)] * (count - 1)
    return pl.pallas_call(
        kernel,
        out_shape=out_shape,
        in_specs=in_specs,
        out_specs=[pl.BlockSpec(memory_space=pltpu.VMEM)] * len(out_shape),
        scratch_shapes=scratch,
        compiler_params=pltpu.CompilerParams(vmem_limit_bytes=VMEM_LIMIT),
    )


def window_scratch(lon, lat, rows):
    return [
        vmem((lon, lat, D), F32),
        vmem((lon, lat, D), F32),
        vmem((rows, D), BF),
        vmem((rows, D), BF),
        vmem((rows, 128), F32),
        vmem((rows, 4 * D), BF),
        vmem((rows, D), BF),
        vmem((rows, 3 * D), BF),
    ]


LON = ("zh", "x", "core")
LAT = ("y", "zl")
ALL = LON + LAT


def shift_to(value, d_lon, d_lat):
    pairs = []
    for a in range(16):
        for b in range(8):
            pairs.append((a * 8 + b, ((a + d_lon) % 16) * 8 + (b + d_lat) % 8))
    return lax.ppermute(value, ALL, pairs)


def scatter_sum(blocks, axes, count):
    here = lax.axis_index(axes)
    total = lax.dynamic_index_in_dim(blocks, here, 0, keepdims=False).astype(F32)
    for step in range(1, count):
        block = lax.dynamic_index_in_dim(blocks, (here + step) % count, 0, keepdims=False)
        pairs = [(n, (n + step) % count) for n in range(count)]
        total = total + lax.ppermute(block, axes, pairs).astype(F32)
    return total


def bias_lookup(bias_table, rel_index):
    one_hot = (
        rel_index.reshape(-1)[:, None] == jnp.arange(bias_table.shape[1], dtype=jnp.int32)[None, :]
    ).astype(F32)
    rows = jnp.dot(one_hot, bias_table.T, precision=lax.Precision.HIGHEST)
    return rows.reshape(CELLS, CELLS, HEADS).transpose(0, 2, 1).reshape(CELLS, HEADS * CELLS)


def local(tokens, pad_mask, shifts, bias_table, rel_index, w_qkv, w_out, grad_out):
    lon_at = lax.axis_index(LON)
    lat_at = lax.axis_index(LAT)
    core = lax.axis_index("core")
    s0, s1 = shifts[0], shifts[1]

    both = lambda a, b: jnp.concatenate([tokens[a, b], grad_out[a, b]], axis=-1)
    halo_lat = shift_to(both(slice(None), slice(0, 8)), 0, -1)
    halo_lon = shift_to(both(slice(0, 8), slice(None)), -1, 0)
    halo_cor = shift_to(both(slice(0, 8), slice(0, 8)), -1, -1)

    bias = bias_lookup(bias_table, rel_index) * LOG2E
    lon_places = (lon_at * 64 + s0 + jnp.arange(64, dtype=jnp.int32)) % 1024
    lat_places = (lat_at * 32 + s1 + jnp.arange(32, dtype=jnp.int32)) % 256
    valid = jnp.take(jnp.take(pad_mask, lon_places, axis=0), lat_places, axis=1)
    keys = valid.reshape(8, 8, 4, 8).transpose(0, 2, 1, 3).reshape(8, 4, CELLS)
    keys = jnp.concatenate([keys, keys], axis=-1)
    inner_keys = keys[:7, :3].reshape(21, 128)
    edge_keys = jnp.concatenate([keys[:7, 3], keys[7], jnp.zeros((1, 128), jnp.int32)], axis=0)
    thr = jnp.where(lat_at == 7, 8 - s1, 8)
    sc = jnp.stack([s0, s1, core, thr]).astype(jnp.int32)

    updated, tokens_grad, w_first = call(
        interior_kernel,
        [sds((64, 32, D), BF), sds((64, 32, D), BF), sds((D, 4 * D), F32)],
        window_scratch(64, 32, 21 * CELLS),
        7,
    )(sc, tokens, grad_out, inner_keys, bias, w_qkv, w_out)

    edge_lat, edge_lon, out_lat, out_lon, out_cor, w_mine, w_other = call(
        edge_kernel,
        [
            sds((64, 8, 2 * D), BF),
            sds((8, 32, 2 * D), BF),
            sds((64, 8, 2 * D), BF),
            sds((8, 32, 2 * D), BF),
            sds((8, 8, 2 * D), BF),
            sds((D // 2, 4 * D), BF),
            sds((D // 2, 4 * D), BF),
        ],
        window_scratch(72, 32, 12 * CELLS) + [vmem((D, 4 * D), F32)],
        11,
    )(sc, tokens, grad_out, halo_lon, halo_lat, halo_cor, edge_keys, bias, w_qkv, w_out, w_first)

    w_got = lax.ppermute(w_other, "core", [(0, 1), (1, 0)])
    in_lat = shift_to(out_lat, 0, 1)
    in_lon = shift_to(out_lon, 1, 0)
    in_cor = shift_to(out_cor, 1, 1)
    total = (w_mine.astype(F32) + w_got.astype(F32)).astype(BF)
    total = total.reshape(2, 4, 32, 4 * D).transpose(1, 0, 2, 3)
    total = scatter_sum(total, "x", 4).astype(BF)
    total = total.reshape(2, 4, 8, 4 * D).transpose(1, 0, 2, 3)
    total = scatter_sum(total, "y", 4).astype(BF)
    total = scatter_sum(total.reshape(4, 4, 4 * D), ("zh", "zl"), 4)

    updated, tokens_grad = call(
        merge_kernel, [sds((64, 32, D), BF), sds((64, 32, D), BF)], [], 8
    )(sc, updated, tokens_grad, edge_lat, edge_lon, in_lat, in_lon, in_cor)
    return (updated, tokens_grad, total[:, : 3 * D], total[:, 3 * D :])


def solution(mesh):
    fine = Mesh(mesh.devices.reshape(2, 4, 2, 4, 2), ALL)
    in_specs = (P(LON, LAT, None), P(), P(), P(), P(), P(), P(), P(LON, LAT, None))
    out_specs = (P(LON, LAT, None), P(LON, LAT, None), P(ALL, None), P(ALL, None))
    return jax.shard_map(local, mesh=fine, in_specs=in_specs, out_specs=out_specs, check_vma=False)
```

time: 593 us -> 130 us (0.22); the launches traced: 584 us -> 130 us
  waiting for transfers between devices: 235 us -> 22.9 us
  local copies, waits for them, and re-layouts: 137 us -> 10.1 us
  matrix products: 99.6 us -> 2.56 us
  other arithmetic: 79.7 us -> 5.64 us
  Pallas kernels: 0 us -> 59.7 us
  between operations: 22.8 us -> 2.89 us
  starting transfers between devices: 10.5 us -> 25.8 us
    unnamed x2 -> x0, waiting for transfers between devices: 137 us -> none
    dot_general x13 -> x1, matrix products: 99.6 us -> 2.56 us  [bias_lookup(): rows = jnp.dot(one_hot, bias_table.T, precision=lax.Precision.HIGHEST)]
    ppermute x4 -> x16, waiting for transfers between devices: 97.6 us -> 22.9 us  [the longest x9 18.3 us: scatter_sum(): total = total + lax.ppermute(block, axes, pairs).astype(F32)]
    pallas_call x0 -> x3, Pallas kernels: none -> 59.7 us  [the longest x1 32.3 us: local(): call(interior_kernel, [sds((64, 32, D), BF), sds((64, 32, D), BF), sds((D...]
    concatenate x7 -> x6, other arithmetic: 49.9 us -> 1.84 us  [the longest x3 1.01 us: local(): both = lambda a, b: jnp.concatenate([tokens[a, b], grad_out[a, b]], axis=-1)]
    another operation x3 -> x0, local copies, waits for them, and re-layouts: 41.6 us -> none  [the longest x1 24.4 us: attend(): packed.reshape(window_count, window_cells, 4, head_count, head_size)]
    convert_element_type x2 -> x0, local copies, waits for them, and re-layouts: 23.8 us -> none  [the longest x1 16.9 us: attend(): window_grads.reshape(window_count, window_cells, 3 * channels)]
    slice x9 -> x11, local copies, waits for them, and re-layouts: 22.8 us -> 3.9 us  [the longest x8 2.11 us: local(): both = lambda a, b: jnp.concatenate([tokens[a, b], grad_out[a, b]], axis=-1)]
  transfers between devices with their start and end apart: 5 -> 16, of which waited for: 4 -> 8; matrix products, arithmetic and copies ran while one was open for 7% -> 8% of each run, Pallas kernels for 0% -> 30%
where the time goes in v1:
time: 130 us
  Pallas kernels  59.7 us (46%)
  starting transfers between devices  25.8 us (20%)
  waiting for transfers between devices  22.9 us (18%)
  local copies, waits for them, and re-layouts  10.1 us (8%)
  other arithmetic  5.64 us (4%)
  between operations  2.89 us (2%)
  matrix products  2.56 us (2%)
    pallas_call x1, Pallas kernels, local(): call(interior_kernel, [sds((64, 32, D), BF), sds((64, 32, D), BF), sds((D...  32.3 us
    pallas_call x1, Pallas kernels, local(): call(edge_kernel, [sds((64, 8, 2 * D), BF), sds((8, 32, 2 * D), BF), sds(...  21.5 us
    ppermute x9, waiting for transfers between devices, scatter_sum(): total = total + lax.ppermute(block, axes, pairs).astype(F32)  18.3 us
    ppermute x9, starting transfers between devices, scatter_sum(): total = total + lax.ppermute(block, axes, pairs).astype(F32)  14.4 us
    ppermute x6, starting transfers between devices, shift_to(): return lax.ppermute(value, ALL, pairs)  10.8 us
    pallas_call x1, Pallas kernels, local(): call(merge_kernel, [sds((64, 32, D), BF), sds((64, 32, D), BF)], [], 8)  5.9 us
  transfers between devices with their start and end apart: 16, of which 8 were waited for; matrix products, arithmetic and copies ran while one was open for 8% of the time, Pallas kernels for 30%

profile of v1, /device:TPU:0, one launch (start us, length us, event | category | flops | bytes accessed | tf_op | source)
XLA Modules:
  0.0 129.5 jit_solution(338444410191693041)
XLA Ops:
  0.7 1.1 slice.44
  1.8 1.0 slice.43
  2.8 0.9 pad_maximum_fusion.1
  3.6 5.6 %collective-permute-start = (bf16[8,32,1024]{2,1,0:T(8,128)(2,1)}, bf16[8,32,1024]{2,1,0:T(8,128)(2,1)}, u32[]{:S(2)}, u32[]{:S(2)}) collective-permute-start(bf16[8,32,1024]{2,1,0:T(8,128)(2,1)} %pad_maximum_fusion.1), channel_id=1, source_target_pairs={{0,120},{1,121},{2,122},{3,123},{4,124},{5,125},{6,126},{7,127},{8... | collective-permute-start | bytes 1572872 | tf_op jit(solution)/shard_map/ppermute | solution.py:345
  9.4 3.5 %collective-permute-start.1 = (bf16[64,8,1024]{2,1,0:T(8,128)(2,1)S(1)}, bf16[64,8,1024]{2,1,0:T(8,128)(2,1)}, u32[]{:S(2)}, u32[]{:S(2)}) collective-permute-start(bf16[64,8,1024]{2,1,0:T(8,128)(2,1)S(1)} %pad_maximum_fusion), channel_id=1, source_target_pairs={{0,7},{1,0},{2,1},{3,2},{4,3},{5,4},{6,5},{7,6},{8,15},{9,8},{10,9... | collective-permute-start | bytes 3145736 | tf_op jit(solution)/shard_map/ppermute | solution.py:345
  13.0 0.7 collective-permute-start.2
  16.3 0.7 gather_fusion
  18.2 0.6 reshape.168.keys
  18.9 2.6 %convolution_multiply_fusion = f32[4096,8]{0,1:T(8,128)S(1)} fusion(f32[8,225]{1,0:T(8,128)S(1)} %copy-done.10, s32[4096]{0:T(1024)S(1)} %eq.33), kind=kOutput, calls=%fused_computation.2 | convolution fusion | flops 89427968 | bytes 154656 | tf_op jit(solution)/shard_map/dot_general | solution.py:362
  21.7 0.8 mul.39.bias
  22.6 0.7 pad_add_fusion.1.sc
  23.3 32.3 %shard_map.111 = (bf16[64,32,512]{2,1,0:T(8,128)(2,1)}, bf16[64,32,512]{2,1,0:T(8,128)(2,1)}, f32[512,2048]{1,0:T(8,128)}) custom-call(s32[4]{0:T(128)} %pad_add_fusion.1.sc, bf16[64,32,512]{2,1,0:T(8,128)(2,1)} %tokens.3, bf16[64,32,512]{2,1,0:T(8,128)(2,1)} %grads.3, s32[21,128]{1,0:T(8,128)} %reshape.168.keys, f32[64,512]{1,0:T(8,128)} %mul.39.bias, ...), custom_call_target="tpu_custom_call" | custom-call | tf_op jit(solution)/shard_map/pallas_call | solution.py:388
  55.7 0.7 add_add_fusion.keys
  56.4 0.6 copy-done.5
  57.0 21.5 %shard_map.112 = (bf16[64,8,1024]{2,1,0:T(8,128)(2,1)}, bf16[8,32,1024]{2,1,0:T(8,128)(2,1)}, bf16[64,8,1024]{2,1,0:T(8,128)(2,1)}, bf16[8,32,1024]{2,1,0:T(8,12...) custom-call(s32[4]{0:T(128)} %pad_add_fusion.1.sc, ...), custom_call_target="tpu_custom_call" | custom-call | tf_op jit(solution)/shard_map/pallas_call | solution.py:395
  79.0 2.5 %collective-permute-done.6 = bf16[256,2048]{1,0:T(8,128)(2,1)S(1)} collective-permute-done((bf16[256,2048]{1,0:T(8,128)(2,1)}, bf16[256,2048]{1,0:T(8,128)(2,1)S(1)}, u32[]{:S(2)}, u32[]{:S(2)}) %collective-permute-start.6) | collective-permute-done | bytes 1048608 | tf_op jit(solution)/shard_map/ppermute | solution.py:410
  81.5 1.6 %add_convert_fusion = bf16[256,2048]{1,0:T(8,128)(2,1)S(1)} fusion(bf16[256,2048]{1,0:T(8,128)(2,1)S(1)} %collective-permute-done.6, bf16[256,2048]{1,0:T(8,128)(2,1)} %get-tuple-element.26), kind=kLoop, calls=%fused_computation.4 | loop fusion | flops 2097152 | bytes 3145728 | tf_op jit(solution)/shard_map/convert_element_type | solution.py:414
  83.1 0.9 dynamic-slice_bitcast_fusion.2
  84.0 2.0 %collective-permute-start.7 = (bf16[2,32,2048]{2,1,0:T(8,128)(2,1)S(1)}, bf16[2,32,2048]{2,1,0:T(8,128)(2,1)}, u32[]{:S(2)}, u32[]{:S(2)}) collective-permute-start(bf16[2,32,2048]{2,1,0:T(8,128)(2,1)S(1)} %get-tuple-element.28), channel_id=1, source_target_pairs={{0,16},{16,32},{32,48},{48,0},{1,17},{17,33},{33,49},{49,1},{2,18}... | collective-permute-start | bytes 786440 | tf_op jit(solution)/shard_map/ppermute | solution.py:354
  86.0 1.0 collective-permute-start.3
  87.1 6.4 %collective-permute-done.9 = bf16[2,32,2048]{2,1,0:T(8,128)(2,1)} collective-permute-done((bf16[2,32,2048]{2,1,0:T(8,128)(2,1)}, bf16[2,32,2048]{2,1,0:T(8,128)(2,1)}, u32[]{:S(2)}, u32[]{:S(2)}) %collective-permute-start.9) | collective-permute-done | bytes 262176 | tf_op jit(solution)/shard_map/ppermute | solution.py:354
  93.5 1.6 %collective-permute-done.8 = bf16[2,32,2048]{2,1,0:T(8,128)(2,1)} collective-permute-done((bf16[2,32,2048]{2,1,0:T(8,128)(2,1)}, bf16[2,32,2048]{2,1,0:T(8,128)(2,1)}, u32[]{:S(2)}, u32[]{:S(2)}) %collective-permute-start.8) | collective-permute-done | bytes 262176 | tf_op jit(solution)/shard_map/ppermute | solution.py:354
  95.0 5.0 %collective-permute-done.7 = bf16[2,32,2048]{2,1,0:T(8,128)(2,1)} collective-permute-done((bf16[2,32,2048]{2,1,0:T(8,128)(2,1)S(1)}, bf16[2,32,2048]{2,1,0:T(8,128)(2,1)}, u32[]{:S(2)}, u32[]{:S(2)}) %collective-permute-start.7) | collective-permute-done | bytes 262176 | tf_op jit(solution)/shard_map/ppermute | solution.py:354
  100.0 1.2 fusion.4
  101.3 0.8 collective-permute-start.12
  102.5 1.0 collective-permute-start.10
  103.4 2.7 %collective-permute-done.12 = bf16[2,8,2048]{2,1,0:T(8,128)(2,1)S(1)} collective-permute-done((bf16[2,8,2048]{2,1,0:T(8,128)(2,1)S(1)}, bf16[2,8,2048]{2,1,0:T(8,128)(2,1)S(1)}, u32[]{:S(2)}, u32[]{:S(2)}) %collective-permute-start.12) | collective-permute-done | bytes 65568 | tf_op jit(solution)/shard_map/ppermute | solution.py:354
  106.1 2.2 %collective-permute-done.11 = bf16[2,8,2048]{2,1,0:T(8,128)(2,1)S(1)} collective-permute-done((bf16[2,8,2048]{2,1,0:T(8,128)(2,1)S(1)}, bf16[2,8,2048]{2,1,0:T(8,128)(2,1)S(1)}, u32[]{:S(2)}, u32[]{:S(2)}) %collective-permute-start.11) | collective-permute-done | bytes 65568 | tf_op jit(solution)/shard_map/ppermute | solution.py:354
  108.9 8.0 %collective-permute-start.15 = (bf16[4,2048]{1,0:T(4,128)(2,1)S(1)}, bf16[4,2048]{1,0:T(4,128)(2,1)S(1)}, u32[]{:S(2)}, u32[]{:S(2)}) collective-permute-start(bf16[4,2048]{1,0:T(4,128)(2,1)S(1)} %get-tuple-element.35), channel_id=1, source_target_pairs={{0,65},{1,0},{64,1},{65,64},{2,67},{3,2},{66,3},{67,66},{4,69},{5,... | collective-permute-start | bytes 49160 | tf_op jit(solution)/shard_map/ppermute | solution.py:354
  116.9 2.2 %collective-permute-start.14 = (bf16[4,2048]{1,0:T(4,128)(2,1)S(1)}, bf16[4,2048]{1,0:T(4,128)(2,1)S(1)}, u32[]{:S(2)}, u32[]{:S(2)}) collective-permute-start(bf16[4,2048]{1,0:T(4,128)(2,1)S(1)} %get-tuple-element.36), channel_id=1, source_target_pairs={{0,64},{1,65},{64,0},{65,1},{2,66},{3,67},{66,2},{67,3},{4,68},{5,... | collective-permute-start | bytes 49160 | tf_op jit(solution)/shard_map/ppermute | solution.py:354
  119.1 2.0 %collective-permute-done.5.in_cor = bf16[8,8,1024]{2,1,0:T(8,128)(2,1)S(1)} collective-permute-done((bf16[8,8,1024]{2,1,0:T(8,128)(2,1)S(1)}, bf16[8,8,1024]{2,1,0:T(8,128)(2,1)S(1)}, u32[]{:S(2)}, u32[]{:S(2)}) %collective-permute-start.5) | collective-permute-done | bytes 131104 | tf_op jit(solution)/shard_map/ppermute | solution.py:345
  122.4 5.9 %shard_map.113 = (bf16[64,32,512]{2,1,0:T(8,128)(2,1)}, bf16[64,32,512]{2,1,0:T(8,128)(2,1)}) custom-call(s32[4]{0:T(128)} %pad_add_fusion.1.sc, bf16[64,32,512]{2,1,0:T(8,128)(2,1)} %get-tuple-element.16.updated, bf16[64,32,512]{2,1,0:T(8,128)(2,1)} %get-tuple-element.17.tokens_grad, bf16[64,8,1024]{2,1,0:T(8,128)(2,1)} %get-tuple-element.19.edge_lat, ...), custom_call_target="tpu_custom_call" | custom-call | tf_op jit(solution)/shard_map/pallas_call | solution.py:421
  (74 shorter events, 6.5 us)
Async XLA Ops:
  0.6 15.7 %copy-start = (s32[1024,256]{1,0:T(8,128)S(1)}, s32[1024,256]{1,0:T(8,128)}, u32[]{:S(2)}) copy-start(s32[1024,256]{1,0:T(8,128)} %param.9) | copy-start | bytes 3145732
  0.6 8.6 %slice-start.1 = ((bf16[64,32,512]{2,1,0:T(8,128)(2,1)}), bf16[64,8,512]{2,1,0:T(8,128)(2,1)S(1)}, s32[]{:S(2)}) async-start(bf16[64,32,512]{2,1,0:T(8,128)(2,1)} %grads.3), calls=%async_computation.1 | async-start | bytes 1048576 | tf_op jit(solution)/shard_map/slice | solution.py:372
  0.7 8.6 %slice-start = ((bf16[64,32,512]{2,1,0:T(8,128)(2,1)}), bf16[64,8,512]{2,1,0:T(8,128)(2,1)S(1)}, s32[]{:S(2)}) async-start(bf16[64,32,512]{2,1,0:T(8,128)(2,1)} %tokens.3), calls=%async_computation | async-start | bytes 1048576 | tf_op jit(solution)/shard_map/slice | solution.py:372
  2.8 10.2 %copy-start.2 = (bf16[64,32,512]{2,1,0:T(8,128)(2,1)S(1)}, bf16[64,32,512]{2,1,0:T(8,128)(2,1)}, u32[]{:S(2)}) copy-start(bf16[64,32,512]{2,1,0:T(8,128)(2,1)} %grads.3) | copy-start | bytes 6291460
  3.6 9.3 %copy-start.1 = (bf16[64,32,512]{2,1,0:T(8,128)(2,1)S(1)}, bf16[64,32,512]{2,1,0:T(8,128)(2,1)}, u32[]{:S(2)}) copy-start(bf16[64,32,512]{2,1,0:T(8,128)(2,1)} %tokens.3) | copy-start | bytes 6291460
  3.6 52.7 %collective-permute-start = (bf16[8,32,1024]{2,1,0:T(8,128)(2,1)}, bf16[8,32,1024]{2,1,0:T(8,128)(2,1)}, u32[]{:S(2)}, u32[]{:S(2)}) collective-permute-start(bf16[8,32,1024]{2,1,0:T(8,128)(2,1)} %pad_maximum_fusion.1), channel_id=1, source_target_pairs={{0,120},{1,121},{2,122},{3,123},{4,124},{5,125},{6,126},{7,127},{8... | collective-permute-start | bytes 1572872 | tf_op jit(solution)/shard_map/ppermute | solution.py:345
  9.2 4.4 %copy-start.8 = (s32[2]{0:T(128)S(1)}, s32[2]{0:T(128)}, u32[]{:S(2)}) copy-start(s32[2]{0:T(128)} %param.10) | copy-start | bytes 28
  9.2 9.5 %copy-start.7 = (s32[64,64]{1,0:T(8,128)S(1)}, s32[64,64]{1,0:T(8,128)}, u32[]{:S(2)}) copy-start(s32[64,64]{1,0:T(8,128)} %param.12) | copy-start | bytes 49156
  9.2 9.6 %copy-start.10 = (f32[8,225]{1,0:T(8,128)S(1)}, f32[8,225]{1,0:T(8,128)}, u32[]{:S(2)}) copy-start(f32[8,225]{1,0:T(8,128)} %param.11) | copy-start | bytes 21604
  9.4 47.0 %collective-permute-start.1 = (bf16[64,8,1024]{2,1,0:T(8,128)(2,1)S(1)}, bf16[64,8,1024]{2,1,0:T(8,128)(2,1)}, u32[]{:S(2)}, u32[]{:S(2)}) collective-permute-start(bf16[64,8,1024]{2,1,0:T(8,128)(2,1)S(1)} %pad_maximum_fusion), channel_id=1, source_target_pairs={{0,7},{1,0},{2,1},{3,2},{4,3},{5,4},{6,5},{7,6},{8,15},{9,8},{10,9... | collective-permute-start | bytes 3145736 | tf_op jit(solution)/shard_map/ppermute | solution.py:345
  13.0 43.4 %collective-permute-start.2 = (bf16[8,8,1024]{2,1,0:T(8,128)(2,1)S(1)}, bf16[8,8,1024]{2,1,0:T(8,128)(2,1)S(1)}, u32[]{:S(2)}, u32[]{:S(2)}) collective-permute-start(bf16[8,8,1024]{2,1,0:T(8,128)(2,1)S(1)} %pad_maximum_fusion.2), channel_id=1, source_target_pairs={{0,127},{1,120},{2,121},{3,122},{4,123},{5,124},{6,125},{7,126},{8... | collective-permute-start | bytes 393224 | tf_op jit(solution)/shard_map/ppermute | solution.py:345
  56.4 0.6 copy-start.5
  78.5 3.0 %collective-permute-start.6 = (bf16[256,2048]{1,0:T(8,128)(2,1)}, bf16[256,2048]{1,0:T(8,128)(2,1)S(1)}, u32[]{:S(2)}, u32[]{:S(2)}) collective-permute-start(bf16[256,2048]{1,0:T(8,128)(2,1)} %get-tuple-element.27), channel_id=1, source_target_pairs={{0,8},{8,0},{1,9},{9,1},{2,10},{10,2},{3,11},{11,3},{4,12},{12,4},... | collective-permute-start | bytes 3145736 | tf_op jit(solution)/shard_map/ppermute | solution.py:410
  83.1 23.0 %copy-start.9 = (bf16[8,8,1024]{2,1,0:T(8,128)(2,1)S(1)}, bf16[8,8,1024]{2,1,0:T(8,128)(2,1)}, u32[]{:S(2)}) copy-start(bf16[8,8,1024]{2,1,0:T(8,128)(2,1)} %get-tuple-element.23) | copy-start | bytes 393220
  84.0 9.5 %collective-permute-start.9 = (bf16[2,32,2048]{2,1,0:T(8,128)(2,1)}, bf16[2,32,2048]{2,1,0:T(8,128)(2,1)}, u32[]{:S(2)}, u32[]{:S(2)}) collective-permute-start(bf16[2,32,2048]{2,1,0:T(8,128)(2,1)} %get-tuple-element.29), channel_id=1, source_target_pairs={{0,48},{16,0},{32,16},{48,32},{1,49},{17,1},{33,17},{49,33},{2,50}... | collective-permute-start | bytes 786440 | tf_op jit(solution)/shard_map/ppermute | solution.py:354
  84.0 11.0 %collective-permute-start.8 = (bf16[2,32,2048]{2,1,0:T(8,128)(2,1)}, bf16[2,32,2048]{2,1,0:T(8,128)(2,1)}, u32[]{:S(2)}, u32[]{:S(2)}) collective-permute-start(bf16[2,32,2048]{2,1,0:T(8,128)(2,1)} %get-tuple-element.30), channel_id=1, source_target_pairs={{0,32},{16,48},{32,0},{48,16},{1,33},{17,49},{33,1},{49,17},{2,34}... | collective-permute-start | bytes 786440 | tf_op jit(solution)/shard_map/ppermute | solution.py:354
  84.0 16.0 %collective-permute-start.7 = (bf16[2,32,2048]{2,1,0:T(8,128)(2,1)S(1)}, bf16[2,32,2048]{2,1,0:T(8,128)(2,1)}, u32[]{:S(2)}, u32[]{:S(2)}) collective-permute-start(bf16[2,32,2048]{2,1,0:T(8,128)(2,1)S(1)} %get-tuple-element.28), channel_id=1, source_target_pairs={{0,16},{16,32},{32,48},{48,0},{1,17},{17,33},{33,49},{49,1},{2,18}... | collective-permute-start | bytes 786440 | tf_op jit(solution)/shard_map/ppermute | solution.py:354
  86.0 35.1 %collective-permute-start.3 = (bf16[64,8,1024]{2,1,0:T(8,128)(2,1)}, bf16[64,8,1024]{2,1,0:T(8,128)(2,1)S(1)}, u32[]{:S(2)}, u32[]{:S(2)}) collective-permute-start(bf16[64,8,1024]{2,1,0:T(8,128)(2,1)} %get-tuple-element.21), channel_id=1, source_target_pairs={{0,1},{1,2},{2,3},{3,4},{4,5},{5,6},{6,7},{7,0},{8,9},{9,10},{10,1... | collective-permute-start | bytes 3145736 | tf_op jit(solution)/shard_map/ppermute | solution.py:345
  101.3 4.8 %collective-permute-start.12 = (bf16[2,8,2048]{2,1,0:T(8,128)(2,1)S(1)}, bf16[2,8,2048]{2,1,0:T(8,128)(2,1)S(1)}, u32[]{:S(2)}, u32[]{:S(2)}) collective-permute-start(bf16[2,8,2048]{2,1,0:T(8,128)(2,1)S(1)} %get-tuple-element.32), channel_id=1, source_target_pairs={{0,6},{2,0},{4,2},{6,4},{1,7},{3,1},{5,3},{7,5},{8,14},{10,8},{12,... | collective-permute-start | bytes 196616 | tf_op jit(solution)/shard_map/ppermute | solution.py:354
  102.1 6.2 %collective-permute-start.11 = (bf16[2,8,2048]{2,1,0:T(8,128)(2,1)S(1)}, bf16[2,8,2048]{2,1,0:T(8,128)(2,1)S(1)}, u32[]{:S(2)}, u32[]{:S(2)}) collective-permute-start(bf16[2,8,2048]{2,1,0:T(8,128)(2,1)S(1)} %get-tuple-element.33), channel_id=1, source_target_pairs={{0,4},{2,6},{4,0},{6,2},{1,5},{3,7},{5,1},{7,3},{8,12},{10,14},{12... | collective-permute-start | bytes 196616 | tf_op jit(solution)/shard_map/ppermute | solution.py:354
  102.5 6.3 %collective-permute-start.10 = (bf16[2,8,2048]{2,1,0:T(8,128)(2,1)S(1)}, bf16[2,8,2048]{2,1,0:T(8,128)(2,1)S(1)}, u32[]{:S(2)}, u32[]{:S(2)}) collective-permute-start(bf16[2,8,2048]{2,1,0:T(8,128)(2,1)S(1)} %get-tuple-element.31), channel_id=1, source_target_pairs={{0,2},{2,4},{4,6},{6,0},{1,3},{3,5},{5,7},{7,1},{8,10},{10,12},{12... | collective-permute-start | bytes 196616 | tf_op jit(solution)/shard_map/ppermute | solution.py:354
  103.4 17.7 %collective-permute-start.4 = (bf16[8,32,1024]{2,1,0:T(8,128)(2,1)}, bf16[8,32,1024]{2,1,0:T(8,128)(2,1)S(1)}, u32[]{:S(2)}, u32[]{:S(2)}) collective-permute-start(bf16[8,32,1024]{2,1,0:T(8,128)(2,1)} %get-tuple-element.22), channel_id=1, source_target_pairs={{0,8},{1,9},{2,10},{3,11},{4,12},{5,13},{6,14},{7,15},{8,16},{9,17... | collective-permute-start | bytes 1572872 | tf_op jit(solution)/shard_map/ppermute | solution.py:345
  106.1 15.1 %collective-permute-start.5 = (bf16[8,8,1024]{2,1,0:T(8,128)(2,1)S(1)}, bf16[8,8,1024]{2,1,0:T(8,128)(2,1)S(1)}, u32[]{:S(2)}, u32[]{:S(2)}) collective-permute-start(bf16[8,8,1024]{2,1,0:T(8,128)(2,1)S(1)} %copy-done.9), channel_id=1, source_target_pairs={{0,9},{1,10},{2,11},{3,12},{4,13},{5,14},{6,15},{7,8},{8,17},{9,18... | collective-permute-start | bytes 393224 | tf_op jit(solution)/shard_map/ppermute | solution.py:345
  108.9 19.4 %collective-permute-start.15 = (bf16[4,2048]{1,0:T(4,128)(2,1)S(1)}, bf16[4,2048]{1,0:T(4,128)(2,1)S(1)}, u32[]{:S(2)}, u32[]{:S(2)}) collective-permute-start(bf16[4,2048]{1,0:T(4,128)(2,1)S(1)} %get-tuple-element.35), channel_id=1, source_target_pairs={{0,65},{1,0},{64,1},{65,64},{2,67},{3,2},{66,3},{67,66},{4,69},{5,... | collective-permute-start | bytes 49160 | tf_op jit(solution)/shard_map/ppermute | solution.py:354
  116.9 11.4 %collective-permute-start.14 = (bf16[4,2048]{1,0:T(4,128)(2,1)S(1)}, bf16[4,2048]{1,0:T(4,128)(2,1)S(1)}, u32[]{:S(2)}, u32[]{:S(2)}) collective-permute-start(bf16[4,2048]{1,0:T(4,128)(2,1)S(1)} %get-tuple-element.36), channel_id=1, source_target_pairs={{0,64},{1,65},{64,0},{65,1},{2,66},{3,67},{66,2},{67,3},{4,68},{5,... | collective-permute-start | bytes 49160 | tf_op jit(solution)/shard_map/ppermute | solution.py:354
  121.2 0.7 copy-start.6
  121.2 7.1 %collective-permute-start.13 = (bf16[4,2048]{1,0:T(4,128)(2,1)S(1)}, bf16[4,2048]{1,0:T(4,128)(2,1)S(1)}, u32[]{:S(2)}, u32[]{:S(2)}) collective-permute-start(bf16[4,2048]{1,0:T(4,128)(2,1)S(1)} %get-tuple-element.34), channel_id=1, source_target_pairs={{0,1},{1,64},{64,65},{65,0},{2,3},{3,66},{66,67},{67,2},{4,5},{5,6... | collective-permute-start | bytes 49160 | tf_op jit(solution)/shard_map/ppermute | solution.py:354
  121.2 0.8 copy-start.4
  121.2 1.2 copy-start.3

commit v2 on v1

v2 whole, which is shorter than its diff:
```python
import jax
import jax.numpy as jnp
from jax import lax
from jax.experimental import pallas as pl
from jax.experimental.pallas import tpu as pltpu
from jax.sharding import Mesh, PartitionSpec as P

WIN = 8
CELLS = 64
D = 512
HEADS = 8
GROUP = 256
BF = jnp.bfloat16
F32 = jnp.float32
LOG2E = 1.4426950408889634
SCALE = 0.125
VMEM_LIMIT = 56 * 2**20
LON = ("zh", "x", "core")
LAT = ("y", "zl")
ALL = LON + LAT


def dot_nn(a, b):
    return lax.dot_general(a, b, (((1,), (0,)), ((), ())), preferred_element_type=F32)


def dot_nt(a, b):
    return lax.dot_general(a, b, (((1,), (1,)), ((), ())), preferred_element_type=F32)


def dot_tn(a, b):
    return lax.dot_general(a, b, (((0,), (0,)), ((), ())), preferred_element_type=F32)


def iota(shape, dim):
    return lax.broadcasted_iota(jnp.int32, shape, dim)


def load_window(tok, grad, i, j, row, xg, hid, istd):
    x = tok[pl.ds(i, WIN), pl.ds(j, WIN), :].reshape(CELLS, D)
    center = x - jnp.mean(x, axis=-1, keepdims=True)
    inv = lax.rsqrt(jnp.mean(center * center, axis=-1, keepdims=True) + 1e-05)
    hid[pl.ds(row, CELLS), :] = (center * inv).astype(BF)
    istd[pl.ds(row, CELLS), :] = jnp.broadcast_to(inv, (CELLS, 128))
    xg[pl.ds(row, CELLS), :] = grad[pl.ds(i, WIN), pl.ds(j, WIN), :].reshape(CELLS, D).astype(BF)


def project(rows, chunk, hid, xg, w_qkv, w_out, qkvg):
    def step(c, carry):
        at = pl.ds(pl.multiple_of(c * chunk, 64), chunk)
        qkvg[at, : 3 * D] = dot_nn(hid[at, :], w_qkv[...]).astype(BF)
        qkvg[at, 3 * D :] = dot_nt(xg[at, :], w_out[...]).astype(BF)
        return carry

    lax.fori_loop(0, rows // chunk, step, 0)


def attend(first, marks, thrs, bias, qkvg, mix, dq):
    lane = iota((CELLS, 128), 1)
    cell = iota((CELLS, 128), 0)
    diag = (lane & 63) == cell
    block = (iota((GROUP, GROUP), 0) >> 6) == (iota((GROUP, GROUP), 1) >> 6)
    ones = jnp.where(block, 1.0, 0.0).astype(BF)
    zero = jnp.zeros((GROUP, GROUP), BF)
    low_half = lane < 64
    units = []
    for w, (mark, thr) in enumerate(zip(marks, thrs)):
        row = pl.multiple_of((first + w) * CELLS, CELLS)
        same = ((lane & 7) >= thr) == ((cell & 7) >= thr)
        valid = jnp.broadcast_to(mark, (CELLS, 128)) > 0.5
        ok = (valid & same) | diag
        ok = jnp.concatenate([ok, ok], axis=1)
        for h in range(2):
            c = h * GROUP
            at = pl.ds(row, CELLS)
            q = qkvg[at, c : c + GROUP]
            k = qkvg[at, D + c : D + c + GROUP]
            v = qkvg[at, 2 * D + c : 2 * D + c + GROUP]
            g = qkvg[at, 3 * D + c : 3 * D + c + GROUP]
            kbd = jnp.where(block, jnp.concatenate([k] * 4, axis=0), zero)
            vbd = jnp.where(block, jnp.concatenate([v] * 4, axis=0), zero)
            s = dot_nt(q, kbd)
            pg = dot_nt(g, vbd)
            e = jnp.where(ok, jnp.exp2(s * (SCALE * LOG2E) + bias[:, c : c + GROUP]), 0.0)
            units.append((at, c, q, g, kbd, vbd, e, pg))
    total = dot_nn(jnp.concatenate([u[6].astype(BF) for u in units], axis=0), ones)
    probs = []
    for n, u in enumerate(units):
        probs.append(u[6] / total[n * CELLS : (n + 1) * CELLS])
    dots = dot_nn(
        jnp.concatenate([(p * u[7]).astype(BF) for p, u in zip(probs, units)], axis=0), ones
    )
    for n, (at, c, q, g, kbd, vbd, e, pg) in enumerate(units):
        p = probs[n]
        p_low = p.astype(BF)
        ds = (p * (pg - dots[n * CELLS : (n + 1) * CELLS]) * SCALE).astype(BF)
        mix[at, c : c + GROUP] = dot_nn(p_low, vbd).astype(BF)
        dq[at, c : c + GROUP] = dot_nn(ds, kbd).astype(BF)
        for t in range(2):
            lo, hi = t * 128, t * 128 + 128
            kg = dot_tn(ds[:, lo:hi], q[:, lo:hi])
            vg = dot_tn(p_low[:, lo:hi], g[:, lo:hi])
            dq[at, D + c + lo : D + c + hi] = jnp.where(low_half, kg[:64], kg[64:]).astype(BF)
            dq[at, 2 * D + c + lo : 2 * D + c + hi] = jnp.where(low_half, vg[:64], vg[64:]).astype(BF)


def finish_window(tok, grad, i, j, update, normed_grad, hidden, inv):
    at = (pl.ds(i, WIN), pl.ds(j, WIN), slice(None))
    tok[at] = tok[at] + update.reshape(WIN, WIN, D)
    finish_grad(grad, i, j, normed_grad, hidden, inv)


def finish_grad(grad, i, j, normed_grad, hidden, inv):
    at = (pl.ds(i, WIN), pl.ds(j, WIN), slice(None))
    normed = hidden.astype(F32)
    centred = normed_grad - jnp.mean(normed_grad, axis=-1, keepdims=True)
    centred = centred - normed * jnp.mean(normed_grad * normed, axis=-1, keepdims=True)
    grad[at] = grad[at] + (inv * centred).reshape(WIN, WIN, D)


def make_tables(pad_mask, bias_table, rel_index, s0, s1, keys, bias, table, rel):
    base = lax.axis_index(LON) * 64
    first = pad_mask[pl.ds(pl.multiple_of(base, 8), 64), :].astype(F32)
    after = pad_mask[pl.ds(pl.multiple_of((base + 64) & 1023, 8), 8), :].astype(F32)
    rows = pltpu.roll(jnp.concatenate([first, after], axis=0), 72 - s0, 0)[:64]
    lane = iota((256, 512), 1)
    place = (lax.axis_index(LAT) * 32 + s1 + (lane >> 7) * 8 + (lane & 7)) & 255
    pick = jnp.where(iota((256, 512), 0) == place, 1.0, 0.0).astype(BF)
    marks = dot_nn(rows.astype(BF), pick)
    own = (iota((64, 512), 0) & 7) == ((iota((64, 512), 1) & 63) >> 3)
    marks = jnp.sum(jnp.where(own, marks, 0.0).reshape(8, 8, 512), axis=1)
    for b in range(4):
        keys[8 * b : 8 * b + 8, :] = marks[:, 128 * b : 128 * b + 128]

    table[...] = jnp.zeros((8, 256), F32)
    table[:, :225] = bias_table[...] * LOG2E
    rel[:, :64] = rel_index[...]
    rel[:, 64:] = rel_index[...]
    at = rel[...]
    low = at < 128
    at = at & 127
    left = iota((CELLS, 128), 1) < 64
    for pair in range(4):
        found = []
        for h in (2 * pair, 2 * pair + 1):
            half = [
                jnp.take_along_axis(
                    jnp.broadcast_to(table[h : h + 1, c : c + 128], (CELLS, 128)), at, axis=1
                )
                for c in (0, 128)
            ]
            found.append(jnp.where(low, half[0], half[1]))
        bias[:, pair * 128 : pair * 128 + 128] = jnp.where(left, found[0], found[1])


def fill_shifted(s1, src, ref):
    def fill(n, carry):
        at = pl.ds(n * 4, 4)
        ref[at, :, :] = pltpu.roll(src[at, :, :].astype(F32), 32 - s1, 1)
        return carry

    lax.fori_loop(0, 16, fill, 0)


def interior_kernel(
    shifts, tokens, grads, pad_mask, bias_table, rel_index, w_qkv, w_out,
    w_part, mix_out, dq_out, hid_out, istd_out, keys, bias,
    tok, grad, xg, hid, istd, qkvg, mix, dq, table, rel, w_sum, sems,
):
    s0, s1 = shifts[0], shifts[1]
    make_tables(pad_mask, bias_table, rel_index, s0, s1, keys, bias, table, rel)
    fill_shifted(s1, tokens, tok)
    fill_shifted(s1, grads, grad)

    def load(a, carry):
        for b in range(3):
            row = pl.multiple_of((a * 3 + b) * CELLS, CELLS)
            load_window(tok, grad, s0 + a * WIN, b * WIN, row, xg, hid, istd)
        return carry

    lax.fori_loop(0, 7, load, 0)
    project(21 * CELLS, 448, hid, xg, w_qkv, w_out, qkvg)

    def windows(a, carry):
        marks = [keys[pl.ds(8 * b + a, 1), :] for b in range(3)]
        attend(a * 3, marks, [8] * 3, bias, qkvg, mix, dq)
        return carry

    lax.fori_loop(0, 7, windows, 0)
    pairs = ((mix, mix_out), (dq, dq_out), (hid, hid_out), (istd, istd_out))
    copies = [pltpu.make_async_copy(a, b, sems.at[n]) for n, (a, b) in enumerate(pairs)]
    for copy in copies:
        copy.start()
    for b in range(2):
        r = slice(b * 256, (b + 1) * 256)
        w_sum[r, : 3 * D] = dot_tn(hid[:, r], dq[...])
        w_sum[r, 3 * D :] = dot_tn(mix[:, r], xg[...])
        copy = pltpu.make_async_copy(w_sum.at[r], w_part.at[r], sems.at[4 + b])
        copy.start()
        copies.append(copy)
    for copy in copies:
        copy.wait()


def store_interior(s0, s1, ref, edge_lat, edge_lon, out):
    lat = iota((4, 8, D), 1)

    def store(n, carry):
        at = pl.ds(n * 4, 4)
        rows = pltpu.roll(ref[at, :, :], s1, 1)
        last = jnp.where(lat >= s1, edge_lat[at, :, :].astype(F32), rows[:, 24:])
        out[at, :, :] = jnp.concatenate([rows[:, :24], last], axis=1).astype(BF)
        return carry

    lax.fori_loop(0, 16, store, 0)
    mark = (iota((8, 32, D), 0) >= s0) & (iota((8, 32, D), 1) >= s1)
    rows = out[56:64, :, :].astype(F32)
    out[56:64, :, :] = jnp.where(mark, edge_lon[...].astype(F32), rows).astype(BF)


def updated_kernel(shifts, tokens, mix, w_out, edge_lat, edge_lon, out, tok):
    s0, s1 = shifts[0], shifts[1]
    fill_shifted(s1, tokens, tok)

    def finish(a, carry):
        update = dot_nn(mix[pl.ds(pl.multiple_of(a * 192, 64), 192), :], w_out[...])
        for b in range(3):
            at = (pl.ds(s0 + a * WIN, WIN), pl.ds(b * WIN, WIN), slice(None))
            tok[at] = tok[at] + update[b * CELLS : (b + 1) * CELLS].reshape(WIN, WIN, D)
        return carry

    lax.fori_loop(0, 7, finish, 0)
    store_interior(s0, s1, tok, edge_lat, edge_lon, out)


def grad_kernel(shifts, grads, hid, istd, dq, w_qkv, edge_lat, edge_lon, out, grad):
    s0, s1 = shifts[0], shifts[1]
    fill_shifted(s1, grads, grad)

    def finish(a, carry):
        at = pl.ds(pl.multiple_of(a * 192, 64), 192)
        normed_grad = dot_nt(dq[at, :], w_qkv[...])
        hidden, inv = hid[at, :], istd[at, :]
        for b in range(3):
            r = slice(b * CELLS, (b + 1) * CELLS)
            finish_grad(grad, s0 + a * WIN, b * WIN, normed_grad[r], hidden[r], inv[r, :1])
        return carry

    lax.fori_loop(0, 7, finish, 0)
    store_interior(s0, s1, grad, edge_lat, edge_lon, out)


def edge_fill(s1, tokens, grads, halo_lon, halo_lat, halo_cor, tok, grad):
    def fill(n, carry):
        at = pl.ds(n * 8, 8)
        for ref, src, c in ((tok, tokens, 0), (grad, grads, D)):
            rows = [src[at, 24:32, :].astype(F32), halo_lat[at, :, c : c + D].astype(F32)]
            ref[at, 24:32, :] = pltpu.roll(jnp.concatenate(rows, axis=1), 16 - s1, 1)[:, :8]
        return carry

    lax.fori_loop(0, 7, fill, 0)
    for r in range(0, 8, 4):
        for ref, src, c in ((tok, tokens, 0), (grad, grads, D)):
            rows = [src[56 + r : 60 + r], halo_lat[56 + r : 60 + r, :, c : c + D]]
            rows = jnp.concatenate([part.astype(F32) for part in rows], axis=1)
            ref[56 + r : 60 + r] = pltpu.roll(rows, 40 - s1, 1)[:, :32]
            rows = [halo_lon[r : r + 4, :, c : c + D], halo_cor[r : r + 4, :, c : c + D]]
            rows = jnp.concatenate([part.astype(F32) for part in rows], axis=1)
            ref[64 + r : 68 + r] = pltpu.roll(rows, 40 - s1, 1)[:, :32]


def edge_load(s0, tok, grad, xg, hid, istd):
    def load_side(a, carry):
        row = pl.multiple_of(a * CELLS, CELLS)
        load_window(tok, grad, s0 + a * WIN, 24, row, xg, hid, istd)
        return carry

    lax.fori_loop(0, 7, load_side, 0)
    for b in range(4):
        load_window(tok, grad, s0 + 56, b * WIN, (7 + b) * CELLS, xg, hid, istd)


def edge_kernel(
    shifts, tokens, grads, halo_lon, halo_lat, halo_cor, keys, bias, w_qkv, w_out, w_part,
    edge_lat, edge_lon, out_lat, out_lon, out_cor, w_mine, w_other,
    tok, grad, xg, hid, istd, qkvg, mix, dq, w_sum, sem,
):
    s0, s1 = shifts[0], shifts[1]
    core = lax.axis_index("core")
    thr_edge = jnp.where(lax.axis_index(LAT) == 7, 8 - s1, 8)
    w_copy = pltpu.make_async_copy(w_part, w_sum, sem)
    w_copy.start()
    edge_fill(s1, tokens, grads, halo_lon, halo_lat, halo_cor, tok, grad)
    edge_load(s0, tok, grad, xg, hid, istd)
    tail = slice(11 * CELLS, 12 * CELLS)
    xg[tail, :] = jnp.zeros((CELLS, D), BF)
    hid[tail, :] = jnp.zeros((CELLS, D), BF)
    project(12 * CELLS, 384, hid, xg, w_qkv, w_out, qkvg)

    def windows(a, carry):
        seen, thr = [], []
        for w in range(3):
            n = a * 3 + w
            row = jnp.where(n < 7, 24 + n, jnp.minimum(8 * n - 49, 31))
            seen.append(keys[pl.ds(row, 1), :])
            thr.append(jnp.where((n < 7) | (n == 10), thr_edge, 8))
        attend(a * 3, seen, thr, bias, qkvg, mix, dq)
        return carry

    lax.fori_loop(0, 4, windows, 0)
    w_copy.wait()
    for b in range(2):
        r = slice(b * 256, (b + 1) * 256)
        w_sum[r, : 3 * D] += dot_tn(hid[:, r], dq[...])
        w_sum[r, 3 * D :] += dot_tn(mix[:, r], xg[...])

    def split(n, carry):
        to = pl.ds(pl.multiple_of(n * 32, 32), 32)
        w_mine[to, :] = w_sum[pl.ds(pl.multiple_of((2 * n + core) * 32, 32), 32), :].astype(BF)
        w_other[to, :] = w_sum[pl.ds(pl.multiple_of((2 * n + 1 - core) * 32, 32), 32), :].astype(BF)
        return carry

    lax.fori_loop(0, 8, split, 0)

    for base, count in ((0, 4), (4, 4), (8, 3)):
        at = slice(base * CELLS, (base + count) * CELLS)
        update = dot_nn(mix[at, :], w_out[...])
        normed_grad = dot_nt(dq[at, :], w_qkv[...])
        for b in range(count):
            r = slice(b * CELLS, (b + 1) * CELLS)
            rr = slice((base + b) * CELLS, (base + b + 1) * CELLS)
            n = base + b
            a, c = (n, 3) if n < 7 else (7, n - 7)
            finish_window(
                tok, grad, s0 + a * WIN, c * WIN,
                update[r], normed_grad[r], hid[rr, :], istd[rr, :1],
            )

    def store(n, carry):
        at = pl.ds(n * 8, 8)
        for ref, c in ((tok, 0), (grad, D)):
            rows = ref[at, 24:32, :]
            rows = jnp.concatenate([rows, jnp.zeros_like(rows)], axis=1)
            rows = pltpu.roll(rows, s1, 1).astype(BF)
            edge_lat[c // D, at, :, :] = rows[:, :8]
            out_lat[at, :, c : c + D] = rows[:, 8:]
        return carry

    lax.fori_loop(0, 7, store, 0)
    for r in range(0, 8, 4):
        for ref, c in ((tok, 0), (grad, D)):
            cols = slice(c, c + D)
            pad = jnp.zeros((4, 8, D), F32)
            rows = pltpu.roll(jnp.concatenate([ref[56 + r : 60 + r], pad], axis=1), s1, 1)
            rows = rows.astype(BF)
            edge_lon[c // D, r : r + 4, :, :] = rows[:, :32]
            edge_lat[c // D, 56 + r : 60 + r, :, :] = rows[:, 24:32]
            out_lat[56 + r : 60 + r, :, cols] = rows[:, 32:]
            rows = pltpu.roll(jnp.concatenate([ref[64 + r : 68 + r], pad], axis=1), s1, 1)
            rows = rows.astype(BF)
            out_lon[r : r + 4, :, cols] = rows[:, :32]
            out_cor[r : r + 4, :, cols] = rows[:, 32:]


def return_kernel(
    shifts, updated, tokens_grad, in_lat, in_lon, in_cor, out_updated, out_grad, side, top, sems
):
    s0, s1 = shifts[0], shifts[1]
    outs = (out_updated, out_grad)
    into = []
    for n, out in enumerate(outs):
        into.append(pltpu.make_async_copy(out.at[:, 0:16, :], side.at[n], sems.at[2 * n]))
        into.append(pltpu.make_async_copy(out.at[0:8, 16:32, :], top.at[n], sems.at[2 * n + 1]))
    for copy in into:
        copy.start()
    for copy in into:
        copy.wait()
    lat = iota((8, 8, D), 1)
    lon = iota((8, 8, D), 0)
    pick = lambda mark, new, old: jnp.where(mark, new.astype(F32), old)
    for n in range(2):
        cols = slice(n * D, n * D + D)

        def rest(r, carry, n=n, cols=cols):
            at = pl.ds(pl.multiple_of(r * 8, 8), 8)
            rows = side[n, at, 0:8, :].astype(F32)
            side[n, at, 0:8, :] = pick(lat < s1, in_lat[at, :, cols], rows).astype(BF)
            return carry

        lax.fori_loop(1, 8, rest, 0)
        rows = side[n, 0:8, 0:8, :].astype(F32)
        rows = pick((lat < s1) & (lon >= s0), in_lat[0:8, :, cols], rows)
        rows = pick((lat >= s1) & (lon < s0), in_lon[:, 0:8, cols], rows)
        rows = pick((lat < s1) & (lon < s0), in_cor[:, :, cols], rows)
        side[n, 0:8, 0:8, :] = rows.astype(BF)
        rows = side[n, 0:8, 8:16, :].astype(F32)
        side[n, 0:8, 8:16, :] = pick(lon < s0, in_lon[:, 8:16, cols], rows).astype(BF)
        rows = top[n].astype(F32)
        top[n] = pick(iota((8, 16, D), 0) < s0, in_lon[:, 16:32, cols], rows).astype(BF)
    back = []
    for n, out in enumerate(outs):
        back.append(pltpu.make_async_copy(side.at[n], out.at[:, 0:16, :], sems.at[2 * n]))
        back.append(pltpu.make_async_copy(top.at[n], out.at[0:8, 16:32, :], sems.at[2 * n + 1]))
    for copy in back:
        copy.start()
    for copy in back:
        copy.wait()


def vmem(shape, dtype):
    return pltpu.VMEM(shape, dtype)


def sds(shape, dtype):
    return jax.ShapeDtypeStruct(shape, dtype)


IN_VMEM = pl.BlockSpec(memory_space=pltpu.VMEM)
IN_SMEM = pl.BlockSpec(memory_space=pltpu.SMEM)
IN_HBM = pl.BlockSpec(memory_space=pl.ANY)


def call(kernel, out_shape, scratch, in_specs, out_specs, aliases=None):
    return pl.pallas_call(
        kernel,
        out_shape=out_shape,
        in_specs=[IN_SMEM] + in_specs,
        out_specs=out_specs,
        scratch_shapes=scratch,
        input_output_aliases=aliases or {},
        compiler_params=pltpu.CompilerParams(vmem_limit_bytes=VMEM_LIMIT),
    )


def window_scratch(lon, lat, rows):
    return [
        vmem((lon, lat, D), F32),
        vmem((lon, lat, D), F32),
        vmem((rows, D), BF),
        vmem((rows, D), BF),
        vmem((rows, 128), F32),
    ]


def attend_scratch(rows):
    return [
        vmem((rows, 4 * D), BF),
        vmem((rows, D), BF),
        vmem((rows, 3 * D), BF),
    ]


def shift_to(value, d_lon, d_lat):
    pairs = []
    for a in range(16):
        for b in range(8):
            pairs.append((a * 8 + b, ((a + d_lon) % 16) * 8 + (b + d_lat) % 8))
    return lax.ppermute(value, ALL, pairs)


def scatter_sum(blocks, axes, count, beside=None):
    here = lax.axis_index(axes)
    parts = [lax.dynamic_index_in_dim(blocks, here, 0, keepdims=False)]
    for step in range(1, count):
        block = lax.dynamic_index_in_dim(blocks, (here + step) % count, 0, keepdims=False)
        pairs = [(n, (n + step) % count) for n in range(count)]
        parts.append(lax.ppermute(block, axes, pairs))
    extra = None
    if beside is not None:
        extra = beside(blocks)
        *parts, extra = lax.optimization_barrier((*parts, extra))
    total = parts[0].astype(F32)
    for part in parts[1:]:
        total = total + part.astype(F32)
    return total, extra


def local(tokens, pad_mask, shifts, bias_table, rel_index, w_qkv, w_out, grad_out):
    both = lambda a, b: jnp.concatenate([tokens[a, b], grad_out[a, b]], axis=-1)
    halo_lat = shift_to(both(slice(None), slice(0, 8)), 0, -1)
    halo_lon = shift_to(both(slice(0, 8), slice(None)), -1, 0)
    halo_cor = shift_to(both(slice(0, 8), slice(0, 8)), -1, -1)
    inner, outer = 21 * CELLS, 12 * CELLS
    grid = sds((64, 32, D), BF)
    halos = (halo_lon, halo_lat, halo_cor)

    w_part, mix, dq, hid, istd, keys, bias = call(
        interior_kernel,
        [
            sds((D, 4 * D), F32),
            sds((inner, D), BF),
            sds((inner, 3 * D), BF),
            sds((inner, D), BF),
            sds((inner, 128), F32),
            sds((32, 128), F32),
            sds((64, 512), F32),
        ],
        window_scratch(64, 32, inner)
        + attend_scratch(inner)
        + [vmem((8, 256), F32), vmem((64, 128), jnp.int32), vmem((D, 4 * D), F32), pltpu.SemaphoreType.DMA((6,))],
        [IN_VMEM] * 7,
        [IN_HBM] * 5 + [IN_VMEM] * 2,
    )(shifts, tokens, grad_out, pad_mask, bias_table, rel_index, w_qkv, w_out)

    edge_lat, edge_lon, out_lat, out_lon, out_cor, w_mine, w_other = call(
        edge_kernel,
        [
            sds((2, 64, 8, D), BF),
            sds((2, 8, 32, D), BF),
            sds((64, 8, 2 * D), BF),
            sds((8, 32, 2 * D), BF),
            sds((8, 8, 2 * D), BF),
            sds((D // 2, 4 * D), BF),
            sds((D // 2, 4 * D), BF),
        ],
        window_scratch(72, 32, outer)
        + attend_scratch(outer)
        + [vmem((D, 4 * D), F32), pltpu.SemaphoreType.DMA],
        [IN_VMEM] * 9 + [IN_HBM],
        [IN_VMEM] * 7,
    )(shifts, tokens, grad_out, *halos, keys, bias, w_qkv, w_out, w_part)

    def grad_beside(blocks):
        _, rows = lax.optimization_barrier((blocks, dq))
        return call(grad_kernel, grid, [vmem((64, 32, D), F32)], [IN_VMEM] * 7, IN_VMEM)(
            shifts, grad_out, hid, istd, rows, w_qkv, edge_lat[1], edge_lon[1]
        )

    def updated_beside(blocks):
        _, rows = lax.optimization_barrier((blocks, mix))
        return call(updated_kernel, grid, [vmem((64, 32, D), F32)], [IN_VMEM] * 5, IN_VMEM)(
            shifts, tokens, rows, w_out, edge_lat[0], edge_lon[0]
        )

    w_got = lax.ppermute(w_other, "core", [(0, 1), (1, 0)])
    in_lat = shift_to(out_lat, 0, 1)
    in_lon = shift_to(out_lon, 1, 0)
    in_cor = shift_to(out_cor, 1, 1)
    total = (w_mine.astype(F32) + w_got.astype(F32)).astype(BF)
    total = total.reshape(2, 4, 32, 4 * D).transpose(1, 0, 2, 3)
    total, tokens_grad = scatter_sum(total, "x", 4, grad_beside)
    total = total.astype(BF).reshape(2, 4, 8, 4 * D).transpose(1, 0, 2, 3)
    total, updated = scatter_sum(total, "y", 4, updated_beside)
    total, _ = scatter_sum(total.astype(BF).reshape(4, 4, 4 * D), ("zh", "zl"), 4)

    updated, tokens_grad = call(
        return_kernel,
        [grid, grid],
        [vmem((2, 64, 16, D), BF), vmem((2, 8, 16, D), BF), pltpu.SemaphoreType.DMA((4,))],
        [IN_HBM] * 2 + [IN_VMEM] * 3,
        [IN_HBM] * 2,
        {1: 0, 2: 1},
    )(shifts, updated, tokens_grad, in_lat, in_lon, in_cor)
    return (updated, tokens_grad, total[:, : 3 * D], total[:, 3 * D :])


def solution(mesh):
    fine = Mesh(mesh.devices.reshape(2, 4, 2, 4, 2), ALL)
    in_specs = (P(LON, LAT, None), P(), P(), P(), P(), P(), P(), P(LON, LAT, None))
    out_specs = (P(LON, LAT, None), P(LON, LAT, None), P(ALL, None), P(ALL, None))
    return jax.shard_map(local, mesh=fine, in_specs=in_specs, out_specs=out_specs, check_vma=False)
```

time: 130 us -> 113 us (0.87)
  waiting for transfers between devices: 22.9 us -> 3.56 us
  Pallas kernels: 59.7 us -> 69.1 us
  other arithmetic: 5.64 us -> 2.1 us
  matrix products: 2.56 us -> 0 us
  starting transfers between devices: 25.8 us -> 28.1 us
  between operations: 2.89 us -> 1.01 us
  local copies, waits for them, and re-layouts: 10.1 us -> 8.42 us
    ppermute x9, waiting for transfers between devices: 18.3 us -> 0.02 us  [scatter_sum(): parts.append(lax.ppermute(block, axes, pairs))]
    pallas_call x3 -> x5, Pallas kernels: 59.7 us -> 69.1 us  [the longest x1 24.5 us: local(): call(interior_kernel, [sds((D, 4 * D), F32), sds((inner, D), BF), sds((in...]
    ppermute x6, starting transfers between devices: 10.8 us -> 14.1 us  [shift_to(): return lax.ppermute(value, ALL, pairs)]
    squeeze x0 -> x2, local copies, waits for them, and re-layouts: none -> 2.88 us  [the longest x1 1.86 us: updated_beside(): edge_lon[0]]
    dot_general x1 -> x0, matrix products: 2.56 us -> none  [bias_lookup(): rows = jnp.dot(one_hot, bias_table.T, precision=lax.Precision.HIGHEST)]
    ppermute x1, waiting for transfers between devices: 2.5 us -> 0.01 us  [local(): w_got = lax.ppermute(w_other, 'core', [(0, 1), (1, 0)])]
    ppermute x6, waiting for transfers between devices: 2.06 us -> 3.53 us  [shift_to(): return lax.ppermute(value, ALL, pairs)]
    gather x4 -> x0, local copies, waits for them, and re-layouts: 1.43 us -> none  [local(): valid = jnp.take(jnp.take(pad_mask, lon_places, axis=0), lat_places, axis=1)]
  transfers between devices with their start and end apart: 16 -> 16, of which waited for: 8 -> 1; matrix products, arithmetic and copies ran while one was open for 8% -> 4% of each run, Pallas kernels for 30% -> 44%
where the time goes in v2:
time: 113 us; the launch traced here: 112 us
  Pallas kernels  69.1 us (61%)
  starting transfers between devices  28.1 us (25%)
  local copies, waits for them, and re-layouts  8.42 us (7%)
  waiting for transfers between devices  3.56 us (3%)
  other arithmetic  2.1 us (2%)
    pallas_call x1, Pallas kernels, local(): call(interior_kernel, [sds((D, 4 * D), F32), sds((inner, D), BF), sds((in...  24.5 us
    pallas_call x1, Pallas kernels, local(): call(edge_kernel, [sds((2, 64, 8, D), BF), sds((2, 8, 32, D), BF), sds((6...  20.3 us
    ppermute x6, starting transfers between devices, shift_to(): return lax.ppermute(value, ALL, pairs)  14.1 us
    ppermute x9, starting transfers between devices, scatter_sum(): parts.append(lax.ppermute(block, axes, pairs))  13.9 us
    pallas_call x1, Pallas kernels, grad_beside(): call(grad_kernel, grid, [vmem((64, 32, D), F32)], [IN_VMEM] * 7, IN_VMEM)  12.4 us
    pallas_call x1, Pallas kernels, updated_beside(): call(updated_kernel, grid, [vmem((64, 32, D), F32)], [IN_VMEM] * 5, IN_VMEM)  7.15 us
    pallas_call x1, Pallas kernels, local(): call(return_kernel, [grid, grid], [vmem((2, 64, 16, D), BF), vmem((2, 8,...  4.79 us
    ppermute x6, waiting for transfers between devices, shift_to(): return lax.ppermute(value, ALL, pairs)  3.53 us
  transfers between devices with their start and end apart: 16, of which 1 were waited for; matrix products, arithmetic and copies ran while one was open for 4% of the time, Pallas kernels for 44%

profile of v2, /device:TPU:0, one launch (start us, length us, event | category | flops | bytes accessed | tf_op | source)
XLA Modules:
  0.0 112.3 jit_solution(5328207432291066567)
XLA Ops:
  0.7 1.0 slice-done
  1.7 0.2 slice-done.2
  1.8 0.1 pad_maximum_fusion
  2.0 4.5 %collective-permute-start.1 = (bf16[64,8,1024]{2,1,0:T(8,128)(2,1)S(1)}, bf16[64,8,1024]{2,1,0:T(8,128)(2,1)S(1)}, u32[]{:S(2)}, u32[]{:S(2)}) collective-permute-start(bf16[64,8,1024]{2,1,0:T(8,128)(2,1)S(1)} %pad_maximum_fusion), channel_id=1, source_target_pairs={{0,7},{1,0},{2,1},{3,2},{4,3},{5,4},{6,5},{7,6},{8,15},{9,8},{10,9... | collective-permute-start | bytes 3145736 | tf_op jit(solution)/shard_map/ppermute | solution.py:458
  6.6 5.0 %collective-permute-start = (bf16[8,32,1024]{2,1,0:T(8,128)(2,1)S(1)}, bf16[8,32,1024]{2,1,0:T(8,128)(2,1)S(1)}, u32[]{:S(2)}, u32[]{:S(2)}) collective-permute-start(bf16[8,32,1024]{2,1,0:T(8,128)(2,1)S(1)} %pad_maximum_fusion.1), channel_id=1, source_target_pairs={{0,120},{1,121},{2,122},{3,123},{4,124},{5,125},{6,126},{7,127},{8... | collective-permute-start | bytes 1572872 | tf_op jit(solution)/shard_map/ppermute | solution.py:458
  11.6 0.8 collective-permute-start.2
  12.4 24.5 %shard_map.111 = (f32[512,2048]{1,0:T(8,128)}, bf16[1344,512]{1,0:T(8,128)(2,1)}, bf16[1344,1536]{1,0:T(8,128)(2,1)}, bf16[1344,512]{1,0:T(8,128)(2,1)}, f32[134...) custom-call(s32[2]{0:T(128)} %shifts.9, bf16[64,32,512]{2,1,0:T(8,128)(2,1)} %tokens.5, ...), custom_call_target="tpu_custom_call" | custom-call | tf_op jit(solution)/shard_map/pallas_call | solution.py:487
  37.0 0.6 copy-done.7
  37.6 0.2 copy-done.6
  37.8 0.3 copy-done.2
  38.1 20.3 %shard_map.112 = (bf16[2,64,8,512]{3,2,1,0:T(8,128)(2,1)}, bf16[2,8,32,512]{3,2,1,0:T(8,128)(2,1)}, bf16[64,8,1024]{2,1,0:T(8,128)(2,1)}, bf16[8,32,1024]{2,1,0:...) custom-call(s32[2]{0:T(128)} %shifts.9, ...), custom_call_target="tpu_custom_call" | custom-call | tf_op jit(solution)/shard_map/pallas_call | solution.py:505
  58.6 1.4 %collective-permute-start.10 = (bf16[64,8,1024]{2,1,0:T(8,128)(2,1)}, bf16[64,8,1024]{2,1,0:T(8,128)(2,1)S(1)}, u32[]{:S(2)}, u32[]{:S(2)}) collective-permute-start(bf16[64,8,1024]{2,1,0:T(8,128)(2,1)} %get-tuple-element.47), channel_id=1, source_target_pairs={{0,1},{1,2},{2,3},{3,4},{4,5},{5,6},{6,7},{7,0},{8,9},{9,10},{10,1... | collective-permute-start | bytes 3145736 | tf_op jit(solution)/shard_map/ppermute | solution.py:458
  59.9 1.9 %slice_bitcast_fusion.2 = (bf16[8,32,512]{2,1,0:T(8,128)(2,1)}, bf16[8,32,512]{2,1,0:T(8,128)(2,1)}) fusion(bf16[2,8,32,512]{3,2,1,0:T(8,128)(2,1)} %get-tuple-element.39), kind=kLoop, calls=%fused_computation.7 | loop fusion | bytes 1048576 | tf_op jit(solution)/shard_map/squeeze | solution.py:532
  61.8 1.7 %add_convert_fusion = bf16[256,2048]{1,0:T(8,128)(2,1)S(1)} fusion(bf16[256,2048]{1,0:T(8,128)(2,1)S(1)} %collective-permute-done.3, bf16[256,2048]{1,0:T(8,128)(2,1)} %get-tuple-element.33), kind=kLoop, calls=%fused_computation | loop fusion | flops 2097152 | bytes 3145728 | tf_op jit(solution)/shard_map/convert_element_type | solution.py:539
  63.7 3.0 %collective-permute-start.5 = (bf16[2,32,2048]{2,1,0:T(8,128)(2,1)S(1)}, bf16[2,32,2048]{2,1,0:T(8,128)(2,1)S(1)}, u32[]{:S(2)}, u32[]{:S(2)}) collective-permute-start(bf16[2,32,2048]{2,1,0:T(8,128)(2,1)S(1)} %get-tuple-element.59), channel_id=1, source_target_pairs={{0,32},{16,48},{32,0},{48,16},{1,33},{17,49},{33,1},{49,17},{2,34}... | collective-permute-start | bytes 786440 | tf_op jit(solution)/shard_map/ppermute | solution.py:467
  66.7 0.2 collective-permute-start.6
  66.9 1.0 slice_bitcast_fusion
  67.9 12.4 %shard_map.113.tokens_grad = bf16[64,32,512]{2,1,0:T(8,128)(2,1)} custom-call(s32[2]{0:T(128)} %shifts.9, bf16[64,32,512]{2,1,0:T(8,128)(2,1)} %grads.5, bf16[1344,512]{1,0:T(8,128)(2,1)} %get-tuple-element.35.hid, f32[1344,128]{1,0:T(8,128)} %get-tuple-element.36.istd, bf16[1344,1536]{1,0:T(8,128)(2,1)} %get-tuple-element.37.dq, bf16[512,1536]{1,0:T(8,128)(2,1)} %w_qkv.5, ...), custom_call_target="tpu_custom_call" | custom-call | tf_op jit(solution)/shard_map/pallas_call | solution.py:525
  80.4 0.1 fusion
  80.5 1.9 %collective-permute-start.7 = (bf16[2,8,2048]{2,1,0:T(8,128)(2,1)S(1)}, bf16[2,8,2048]{2,1,0:T(8,128)(2,1)S(1)}, u32[]{:S(2)}, u32[]{:S(2)}) collective-permute-start(bf16[2,8,2048]{2,1,0:T(8,128)(2,1)S(1)} %get-tuple-element.66), channel_id=1, source_target_pairs={{0,2},{2,4},{4,6},{6,0},{1,3},{3,5},{5,7},{7,1},{8,10},{10,12},{12... | collective-permute-start | bytes 196616 | tf_op jit(solution)/shard_map/ppermute | solution.py:467
  82.5 3.6 %collective-permute-start.8 = (bf16[2,8,2048]{2,1,0:T(8,128)(2,1)S(1)}, bf16[2,8,2048]{2,1,0:T(8,128)(2,1)S(1)}, u32[]{:S(2)}, u32[]{:S(2)}) collective-permute-start(bf16[2,8,2048]{2,1,0:T(8,128)(2,1)S(1)} %get-tuple-element.65), channel_id=1, source_target_pairs={{0,4},{2,6},{4,0},{6,2},{1,5},{3,7},{5,1},{7,3},{8,12},{10,14},{12... | collective-permute-start | bytes 196616 | tf_op jit(solution)/shard_map/ppermute | solution.py:467
  86.1 1.2 %collective-permute-start.9 = (bf16[2,8,2048]{2,1,0:T(8,128)(2,1)S(1)}, bf16[2,8,2048]{2,1,0:T(8,128)(2,1)S(1)}, u32[]{:S(2)}, u32[]{:S(2)}) collective-permute-start(bf16[2,8,2048]{2,1,0:T(8,128)(2,1)S(1)} %get-tuple-element.64), channel_id=1, source_target_pairs={{0,6},{2,0},{4,2},{6,4},{1,7},{3,1},{5,3},{7,5},{8,14},{10,8},{12,... | collective-permute-start | bytes 196616 | tf_op jit(solution)/shard_map/ppermute | solution.py:467
  87.3 7.2 %shard_map.114.updated = bf16[64,32,512]{2,1,0:T(8,128)(2,1)} custom-call(s32[2]{0:T(128)} %shifts.9, bf16[64,32,512]{2,1,0:T(8,128)(2,1)} %tokens.5, bf16[1344,512]{1,0:T(8,128)(2,1)} %get-tuple-element.44.mix, bf16[512,512]{1,0:T(8,128)(2,1)} %w_out.5, bf16[64,8,512]{2,1,0:T(8,128)(2,1)} %get-tuple-element.56.edge_lat, ...), custom_call_target="tpu_custom_call" | custom-call | tf_op jit(solution)/shard_map/pallas_call | solution.py:531
  94.5 2.5 %collective-permute-start.12 = (bf16[8,8,1024]{2,1,0:T(8,128)(2,1)S(1)}, bf16[8,8,1024]{2,1,0:T(8,128)(2,1)S(1)}, u32[]{:S(2)}, u32[]{:S(2)}) collective-permute-start(bf16[8,8,1024]{2,1,0:T(8,128)(2,1)S(1)} %copy-done.10), channel_id=1, source_target_pairs={{0,9},{1,10},{2,11},{3,12},{4,13},{5,14},{6,15},{7,8},{8,17},{9,18... | collective-permute-start | bytes 393224 | tf_op jit(solution)/shard_map/ppermute | solution.py:458
  97.0 3.8 %collective-permute-start.15 = (bf16[4,2048]{1,0:T(4,128)(2,1)S(1)}, bf16[4,2048]{1,0:T(4,128)(2,1)S(1)}, u32[]{:S(2)}, u32[]{:S(2)}) collective-permute-start(bf16[4,2048]{1,0:T(4,128)(2,1)S(1)} %get-tuple-element.69), channel_id=1, source_target_pairs={{0,65},{1,0},{64,1},{65,64},{2,67},{3,2},{66,3},{67,66},{4,69},{5,... | collective-permute-start | bytes 49160 | tf_op jit(solution)/shard_map/ppermute | solution.py:467
  100.9 3.5 %collective-permute-done.12.in_cor = bf16[8,8,1024]{2,1,0:T(8,128)(2,1)S(1)} collective-permute-done((bf16[8,8,1024]{2,1,0:T(8,128)(2,1)S(1)}, bf16[8,8,1024]{2,1,0:T(8,128)(2,1)S(1)}, u32[]{:S(2)}, u32[]{:S(2)}) %collective-permute-start.12) | collective-permute-done | bytes 131104 | tf_op jit(solution)/shard_map/ppermute | solution.py:458
  104.4 0.6 copy-done.8
  105.0 0.2 copy-done.5
  105.2 1.0 copy-done.4
  106.2 4.8 %shard_map.115 = (bf16[64,32,512]{2,1,0:T(8,128)(2,1)}, bf16[64,32,512]{2,1,0:T(8,128)(2,1)}) custom-call(s32[2]{0:T(128)} %shifts.9, bf16[64,32,512]{2,1,0:T(8,128)(2,1)} %shard_map.114.updated, bf16[64,32,512]{2,1,0:T(8,128)(2,1)} %shard_map.113.tokens_grad, bf16[64,8,1024]{2,1,0:T(8,128)(2,1)} %copy-done.4, ...), custom_call_target="tpu_custom_call", output_to_operand_aliasing={{0}: (1, {}), {1}: (2, {})} | custom-call | tf_op jit(solution)/shard_map/pallas_call | solution.py:546
  111.1 0.6 slice.48
  111.7 0.6 slice.49
  (52 shorter events, 0.6 us)
Async XLA Ops:
  0.6 1.0 slice-start
  0.6 1.2 %slice-start.2 = ((bf16[64,32,512]{2,1,0:T(8,128)(2,1)}), bf16[64,8,512]{2,1,0:T(8,128)(2,1)S(1)}, s32[]{:S(2)}) async-start(bf16[64,32,512]{2,1,0:T(8,128)(2,1)} %tokens.5), calls=%async_computation.2 | async-start | bytes 1048576 | tf_op jit(solution)/shard_map/slice | solution.py:479
  0.7 5.9 %slice-start.1 = ((bf16[64,32,512]{2,1,0:T(8,128)(2,1)}), bf16[8,32,512]{2,1,0:T(8,128)(2,1)S(1)}, s32[]{:S(2)}) async-start(bf16[64,32,512]{2,1,0:T(8,128)(2,1)} %grads.5), calls=%async_computation.1 | async-start | bytes 524288 | tf_op jit(solution)/shard_map/slice | solution.py:479
  0.7 5.8 %slice-start.3 = ((bf16[64,32,512]{2,1,0:T(8,128)(2,1)}), bf16[8,32,512]{2,1,0:T(8,128)(2,1)S(1)}, s32[]{:S(2)}) async-start(bf16[64,32,512]{2,1,0:T(8,128)(2,1)} %tokens.5), calls=%async_computation.3 | async-start | bytes 524288 | tf_op jit(solution)/shard_map/slice | solution.py:479
  1.8 9.7 %copy-start = (bf16[64,32,512]{2,1,0:T(8,128)(2,1)S(1)}, bf16[64,32,512]{2,1,0:T(8,128)(2,1)}, u32[]{:S(2)}) copy-start(bf16[64,32,512]{2,1,0:T(8,128)(2,1)} %grads.5) | copy-start | bytes 6291460
  1.8 9.8 %copy-start.1 = (bf16[64,32,512]{2,1,0:T(8,128)(2,1)S(1)}, bf16[64,32,512]{2,1,0:T(8,128)(2,1)}, u32[]{:S(2)}) copy-start(bf16[64,32,512]{2,1,0:T(8,128)(2,1)} %tokens.5) | copy-start | bytes 6291460
  2.0 35.0 %collective-permute-start.1 = (bf16[64,8,1024]{2,1,0:T(8,128)(2,1)S(1)}, bf16[64,8,1024]{2,1,0:T(8,128)(2,1)S(1)}, u32[]{:S(2)}, u32[]{:S(2)}) collective-permute-start(bf16[64,8,1024]{2,1,0:T(8,128)(2,1)S(1)} %pad_maximum_fusion), channel_id=1, source_target_pairs={{0,7},{1,0},{2,1},{3,2},{4,3},{5,4},{6,5},{7,6},{8,15},{9,8},{10,9... | collective-permute-start | bytes 3145736 | tf_op jit(solution)/shard_map/ppermute | solution.py:458
  6.6 30.4 %collective-permute-start = (bf16[8,32,1024]{2,1,0:T(8,128)(2,1)S(1)}, bf16[8,32,1024]{2,1,0:T(8,128)(2,1)S(1)}, u32[]{:S(2)}, u32[]{:S(2)}) collective-permute-start(bf16[8,32,1024]{2,1,0:T(8,128)(2,1)S(1)} %pad_maximum_fusion.1), channel_id=1, source_target_pairs={{0,120},{1,121},{2,122},{3,123},{4,124},{5,125},{6,126},{7,127},{8... | collective-permute-start | bytes 1572872 | tf_op jit(solution)/shard_map/ppermute | solution.py:458
  11.6 25.3 %collective-permute-start.2 = (bf16[8,8,1024]{2,1,0:T(8,128)(2,1)S(1)}, bf16[8,8,1024]{2,1,0:T(8,128)(2,1)S(1)}, u32[]{:S(2)}, u32[]{:S(2)}) collective-permute-start(bf16[8,8,1024]{2,1,0:T(8,128)(2,1)S(1)} %pad_maximum_fusion.2), channel_id=1, source_target_pairs={{0,127},{1,120},{2,121},{3,122},{4,123},{5,124},{6,125},{7,126},{8... | collective-permute-start | bytes 393224 | tf_op jit(solution)/shard_map/ppermute | solution.py:458
  36.9 0.6 copy-start.7
  37.0 0.8 copy-start.6
  37.0 1.1 %copy-start.2 = (bf16[64,8,1024]{2,1,0:T(8,128)(2,1)}, bf16[64,8,1024]{2,1,0:T(8,128)(2,1)S(1)}, u32[]{:S(2)}) copy-start(bf16[64,8,1024]{2,1,0:T(8,128)(2,1)S(1)} %collective-permute-done.1.halo_lat) | copy-start | bytes 3145732
  58.4 3.4 %collective-permute-start.3 = (bf16[256,2048]{1,0:T(8,128)(2,1)}, bf16[256,2048]{1,0:T(8,128)(2,1)S(1)}, u32[]{:S(2)}, u32[]{:S(2)}) collective-permute-start(bf16[256,2048]{1,0:T(8,128)(2,1)} %get-tuple-element.34), channel_id=1, source_target_pairs={{0,8},{8,0},{1,9},{9,1},{2,10},{10,2},{3,11},{11,3},{4,12},{12,4},... | collective-permute-start | bytes 3145736 | tf_op jit(solution)/shard_map/ppermute | solution.py:535
  58.6 45.8 %collective-permute-start.10 = (bf16[64,8,1024]{2,1,0:T(8,128)(2,1)}, bf16[64,8,1024]{2,1,0:T(8,128)(2,1)S(1)}, u32[]{:S(2)}, u32[]{:S(2)}) collective-permute-start(bf16[64,8,1024]{2,1,0:T(8,128)(2,1)} %get-tuple-element.47), channel_id=1, source_target_pairs={{0,1},{1,2},{2,3},{3,4},{4,5},{5,6},{6,7},{7,0},{8,9},{9,10},{10,1... | collective-permute-start | bytes 3145736 | tf_op jit(solution)/shard_map/ppermute | solution.py:458
  61.8 5.1 %copy-start.3 = (bf16[2,64,8,512]{3,2,1,0:T(8,128)(2,1)S(1)}, bf16[2,64,8,512]{3,2,1,0:T(8,128)(2,1)}, u32[]{:S(2)}) copy-start(bf16[2,64,8,512]{3,2,1,0:T(8,128)(2,1)} %get-tuple-element.38) | copy-start | bytes 3145732
  63.6 16.7 %collective-permute-start.4 = (bf16[2,32,2048]{2,1,0:T(8,128)(2,1)S(1)}, bf16[2,32,2048]{2,1,0:T(8,128)(2,1)S(1)}, u32[]{:S(2)}, u32[]{:S(2)}) collective-permute-start(bf16[2,32,2048]{2,1,0:T(8,128)(2,1)S(1)} %get-tuple-element.60), channel_id=1, source_target_pairs={{0,16},{16,32},{32,48},{48,0},{1,17},{17,33},{33,49},{49,1},{2,18}... | collective-permute-start | bytes 786440 | tf_op jit(solution)/shard_map/ppermute | solution.py:467
  63.7 16.7 %collective-permute-start.5 = (bf16[2,32,2048]{2,1,0:T(8,128)(2,1)S(1)}, bf16[2,32,2048]{2,1,0:T(8,128)(2,1)S(1)}, u32[]{:S(2)}, u32[]{:S(2)}) collective-permute-start(bf16[2,32,2048]{2,1,0:T(8,128)(2,1)S(1)} %get-tuple-element.59), channel_id=1, source_target_pairs={{0,32},{16,48},{32,0},{48,16},{1,33},{17,49},{33,1},{49,17},{2,34}... | collective-permute-start | bytes 786440 | tf_op jit(solution)/shard_map/ppermute | solution.py:467
  66.7 13.6 %collective-permute-start.6 = (bf16[2,32,2048]{2,1,0:T(8,128)(2,1)S(1)}, bf16[2,32,2048]{2,1,0:T(8,128)(2,1)S(1)}, u32[]{:S(2)}, u32[]{:S(2)}) collective-permute-start(bf16[2,32,2048]{2,1,0:T(8,128)(2,1)S(1)} %get-tuple-element.58), channel_id=1, source_target_pairs={{0,48},{16,0},{32,16},{48,32},{1,49},{17,1},{33,17},{49,33},{2,50}... | collective-permute-start | bytes 786440 | tf_op jit(solution)/shard_map/ppermute | solution.py:467
  67.9 19.4 %copy-start.9 = (bf16[8,32,1024]{2,1,0:T(8,128)(2,1)S(1)}, bf16[8,32,1024]{2,1,0:T(8,128)(2,1)}, u32[]{:S(2)}) copy-start(bf16[8,32,1024]{2,1,0:T(8,128)(2,1)} %get-tuple-element.48) | copy-start | bytes 1572868
  80.5 13.9 %collective-permute-start.7 = (bf16[2,8,2048]{2,1,0:T(8,128)(2,1)S(1)}, bf16[2,8,2048]{2,1,0:T(8,128)(2,1)S(1)}, u32[]{:S(2)}, u32[]{:S(2)}) collective-permute-start(bf16[2,8,2048]{2,1,0:T(8,128)(2,1)S(1)} %get-tuple-element.66), channel_id=1, source_target_pairs={{0,2},{2,4},{4,6},{6,0},{1,3},{3,5},{5,7},{7,1},{8,10},{10,12},{12... | collective-permute-start | bytes 196616 | tf_op jit(solution)/shard_map/ppermute | solution.py:467
  82.5 14.5 %collective-permute-start.8 = (bf16[2,8,2048]{2,1,0:T(8,128)(2,1)S(1)}, bf16[2,8,2048]{2,1,0:T(8,128)(2,1)S(1)}, u32[]{:S(2)}, u32[]{:S(2)}) collective-permute-start(bf16[2,8,2048]{2,1,0:T(8,128)(2,1)S(1)} %get-tuple-element.65), channel_id=1, source_target_pairs={{0,4},{2,6},{4,0},{6,2},{1,5},{3,7},{5,1},{7,3},{8,12},{10,14},{12... | collective-permute-start | bytes 196616 | tf_op jit(solution)/shard_map/ppermute | solution.py:467
  86.1 10.8 %collective-permute-start.9 = (bf16[2,8,2048]{2,1,0:T(8,128)(2,1)S(1)}, bf16[2,8,2048]{2,1,0:T(8,128)(2,1)S(1)}, u32[]{:S(2)}, u32[]{:S(2)}) collective-permute-start(bf16[2,8,2048]{2,1,0:T(8,128)(2,1)S(1)} %get-tuple-element.64), channel_id=1, source_target_pairs={{0,6},{2,0},{4,2},{6,4},{1,7},{3,1},{5,3},{7,5},{8,14},{10,8},{12,... | collective-permute-start | bytes 196616 | tf_op jit(solution)/shard_map/ppermute | solution.py:467
  87.3 17.1 %collective-permute-start.11 = (bf16[8,32,1024]{2,1,0:T(8,128)(2,1)S(1)}, bf16[8,32,1024]{2,1,0:T(8,128)(2,1)S(1)}, u32[]{:S(2)}, u32[]{:S(2)}) collective-permute-start(bf16[8,32,1024]{2,1,0:T(8,128)(2,1)S(1)} %copy-done.9), channel_id=1, source_target_pairs={{0,8},{1,9},{2,10},{3,11},{4,12},{5,13},{6,14},{7,15},{8,16},{9,17... | collective-permute-start | bytes 1572872 | tf_op jit(solution)/shard_map/ppermute | solution.py:458
  87.3 7.2 %copy-start.10 = (bf16[8,8,1024]{2,1,0:T(8,128)(2,1)S(1)}, bf16[8,8,1024]{2,1,0:T(8,128)(2,1)}, u32[]{:S(2)}) copy-start(bf16[8,8,1024]{2,1,0:T(8,128)(2,1)} %get-tuple-element.49) | copy-start | bytes 393220
  94.5 9.9 %collective-permute-start.12 = (bf16[8,8,1024]{2,1,0:T(8,128)(2,1)S(1)}, bf16[8,8,1024]{2,1,0:T(8,128)(2,1)S(1)}, u32[]{:S(2)}, u32[]{:S(2)}) collective-permute-start(bf16[8,8,1024]{2,1,0:T(8,128)(2,1)S(1)} %copy-done.10), channel_id=1, source_target_pairs={{0,9},{1,10},{2,11},{3,12},{4,13},{5,14},{6,15},{7,8},{8,17},{9,18... | collective-permute-start | bytes 393224 | tf_op jit(solution)/shard_map/ppermute | solution.py:458
  97.0 14.0 %collective-permute-start.15 = (bf16[4,2048]{1,0:T(4,128)(2,1)S(1)}, bf16[4,2048]{1,0:T(4,128)(2,1)S(1)}, u32[]{:S(2)}, u32[]{:S(2)}) collective-permute-start(bf16[4,2048]{1,0:T(4,128)(2,1)S(1)} %get-tuple-element.69), channel_id=1, source_target_pairs={{0,65},{1,0},{64,1},{65,64},{2,67},{3,2},{66,3},{67,66},{4,69},{5,... | collective-permute-start | bytes 49160 | tf_op jit(solution)/shard_map/ppermute | solution.py:467
  100.9 10.2 %collective-permute-start.14 = (bf16[4,2048]{1,0:T(4,128)(2,1)S(1)}, bf16[4,2048]{1,0:T(4,128)(2,1)S(1)}, u32[]{:S(2)}, u32[]{:S(2)}) collective-permute-start(bf16[4,2048]{1,0:T(4,128)(2,1)S(1)} %get-tuple-element.70), channel_id=1, source_target_pairs={{0,64},{1,65},{64,0},{65,1},{2,66},{3,67},{66,2},{67,3},{4,68},{5,... | collective-permute-start | bytes 49160 | tf_op jit(solution)/shard_map/ppermute | solution.py:467
  104.4 0.7 copy-start.8
  104.4 6.7 %collective-permute-start.13 = (bf16[4,2048]{1,0:T(4,128)(2,1)S(1)}, bf16[4,2048]{1,0:T(4,128)(2,1)S(1)}, u32[]{:S(2)}, u32[]{:S(2)}) collective-permute-start(bf16[4,2048]{1,0:T(4,128)(2,1)S(1)} %get-tuple-element.68), channel_id=1, source_target_pairs={{0,1},{1,64},{64,65},{65,0},{2,3},{3,66},{66,67},{67,2},{4,5},{5,6... | collective-permute-start | bytes 49160 | tf_op jit(solution)/shard_map/ppermute | solution.py:467
  104.4 0.8 copy-start.5
  105.2 1.0 copy-start.4

commit v3 on v2

v3 whole, which is shorter than its diff:
```python
import jax
import jax.numpy as jnp
from jax import lax
from jax.experimental import pallas as pl
from jax.experimental.pallas import tpu as pltpu
from jax.sharding import Mesh, PartitionSpec as P

WIN = 8
CELLS = 64
D = 512
HEADS = 8
GROUP = 256
BF = jnp.bfloat16
F32 = jnp.float32
LOG2E = 1.4426950408889634
SCALE = 0.125
VMEM_LIMIT = 56 * 2**20
LON = ("zh", "x", "core")
LAT = ("y", "zl")
ALL = LON + LAT


def dot_nn(a, b):
    return lax.dot_general(a, b, (((1,), (0,)), ((), ())), preferred_element_type=F32)


def dot_nt(a, b):
    return lax.dot_general(a, b, (((1,), (1,)), ((), ())), preferred_element_type=F32)


def dot_tn(a, b):
    return lax.dot_general(a, b, (((0,), (0,)), ((), ())), preferred_element_type=F32)


def iota(shape, dim):
    return lax.broadcasted_iota(jnp.int32, shape, dim)


def keep_window(x, g, row, xt, xg, hid, istd):
    at = pl.ds(row, CELLS)
    center = x - jnp.mean(x, axis=-1, keepdims=True)
    inv = lax.rsqrt(jnp.mean(center * center, axis=-1, keepdims=True) + 1e-05)
    hid[at, :] = (center * inv).astype(BF)
    istd[at, :] = jnp.broadcast_to(inv, (CELLS, 128))
    xt[at, :] = x.astype(BF)
    xg[at, :] = g.astype(BF)


def project(rows, chunk, hid, xg, w_qkv, w_out, qkvg):
    def step(c, carry):
        at = pl.ds(pl.multiple_of(c * chunk, 64), chunk)
        qkvg[at, : 3 * D] = dot_nn(hid[at, :], w_qkv[...]).astype(BF)
        qkvg[at, 3 * D :] = dot_nt(xg[at, :], w_out[...]).astype(BF)
        return carry

    lax.fori_loop(0, rows // chunk, step, 0)


def fill_ones(ones):
    block = (iota((GROUP, GROUP), 0) >> 6) == (iota((GROUP, GROUP), 1) >> 6)
    ones[...] = jnp.where(block, 1.0, 0.0).astype(BF)


def attend(first, marks, thrs, bias, ones, qkvg, mix, dq):
    lane = iota((CELLS, 128), 1)
    cell = iota((CELLS, 128), 0)
    diag = (lane & 63) == cell
    low_half = lane < 64
    low_mask = jnp.where(low_half, 1.0, 0.0).astype(BF)
    high_mask = jnp.where(low_half, 0.0, 1.0).astype(BF)
    zero = jnp.zeros((CELLS, 128), BF)

    def by_head(x):
        a, b = x[:, :128], x[:, 128:]
        rows = [(a * low_mask, zero), (a * high_mask, zero), (zero, b * low_mask), (zero, b * high_mask)]
        return jnp.concatenate([jnp.concatenate(r, axis=1) for r in rows], axis=0)

    units = []
    for w, (mark, thr) in enumerate(zip(marks, thrs)):
        row = pl.multiple_of((first + w) * CELLS, CELLS)
        same = ((lane & 7) >= thr) == ((cell & 7) >= thr)
        valid = jnp.broadcast_to(mark, (CELLS, 128)) > 0.5
        ok = (valid & same) | diag
        ok = jnp.concatenate([ok, ok], axis=1)
        for h in range(2):
            c = h * GROUP
            at = pl.ds(row, CELLS)
            q = qkvg[at, c : c + GROUP]
            k = qkvg[at, D + c : D + c + GROUP]
            v = qkvg[at, 2 * D + c : 2 * D + c + GROUP]
            g = qkvg[at, 3 * D + c : 3 * D + c + GROUP]
            kbd, vbd = by_head(k), by_head(v)
            s = dot_nt(q, kbd)
            pg = dot_nt(g, vbd)
            e = jnp.where(ok, jnp.exp2(s * (SCALE * LOG2E) + bias[:, c : c + GROUP]), 0.0)
            units.append((at, c, q, g, kbd, vbd, e, pg))
    total = dot_nn(jnp.concatenate([u[6].astype(BF) for u in units], axis=0), ones[...])
    probs = []
    for n, u in enumerate(units):
        probs.append(u[6] / total[n * CELLS : (n + 1) * CELLS])
    dots = dot_nn(
        jnp.concatenate([(p * u[7]).astype(BF) for p, u in zip(probs, units)], axis=0), ones[...]
    )
    for n, (at, c, q, g, kbd, vbd, e, pg) in enumerate(units):
        p = probs[n]
        p_low = p.astype(BF)
        ds = (p * (pg - dots[n * CELLS : (n + 1) * CELLS]) * SCALE).astype(BF)
        mix[at, c : c + GROUP] = dot_nn(p_low, vbd).astype(BF)
        dq[at, c : c + GROUP] = dot_nn(ds, kbd).astype(BF)
        for t in range(2):
            lo, hi = t * 128, t * 128 + 128
            kg = dot_tn(ds[:, lo:hi], q[:, lo:hi])
            vg = dot_tn(p_low[:, lo:hi], g[:, lo:hi])
            dq[at, D + c + lo : D + c + hi] = jnp.where(low_half, kg[:64], kg[64:]).astype(BF)
            dq[at, 2 * D + c + lo : 2 * D + c + hi] = jnp.where(low_half, vg[:64], vg[64:]).astype(BF)


def finish(at, xt, xg, hid, istd, mix, dq, w_qkv, w_out):
    update = xt[at, :].astype(F32) + dot_nn(mix[at, :], w_out[...])
    normed_grad = dot_nt(dq[at, :], w_qkv[...])
    normed = hid[at, :].astype(F32)
    centred = normed_grad - jnp.mean(normed_grad, axis=-1, keepdims=True)
    centred = centred - normed * jnp.mean(normed_grad * normed, axis=-1, keepdims=True)
    inv = istd[at, :]
    return update, xg[at, :].astype(F32) + jnp.concatenate([inv] * 4, axis=1) * centred


def rows_of(strip):
    return strip.reshape(CELLS, D)


def strip_of(rows, count):
    parts = [rows[n * CELLS : (n + 1) * CELLS].reshape(WIN, WIN, D) for n in range(count)]
    return jnp.concatenate(parts + [jnp.zeros((WIN, WIN, D), F32)], axis=1)


def make_tables(marks_in, bias_table, rel_index, s0, s1, keys, bias, table, rel):
    rows = pltpu.roll(marks_in[...].astype(F32), 72 - s0, 0)[:64]
    lane = iota((256, 512), 1)
    place = (lax.axis_index(LAT) * 32 + s1 + (lane >> 7) * 8 + (lane & 7)) & 255
    pick = jnp.where(iota((256, 512), 0) == place, 1.0, 0.0).astype(BF)
    marks = dot_nn(rows.astype(BF), pick)
    own = (iota((64, 512), 0) & 7) == ((iota((64, 512), 1) & 63) >> 3)
    marks = jnp.sum(jnp.where(own, marks, 0.0).reshape(8, 8, 512), axis=1)
    for b in range(4):
        keys[8 * b : 8 * b + 8, :] = marks[:, 128 * b : 128 * b + 128]

    table[...] = jnp.zeros((8, 256), F32)
    table[:, :225] = bias_table[...] * LOG2E
    rel[:, :64] = rel_index[...]
    rel[:, 64:] = rel_index[...]
    at = rel[...]
    low = at < 128
    at = at & 127
    left = iota((CELLS, 128), 1) < 64
    for pair in range(4):
        found = []
        for h in (2 * pair, 2 * pair + 1):
            half = [
                jnp.take_along_axis(
                    jnp.broadcast_to(table[h : h + 1, c : c + 128], (CELLS, 128)), at, axis=1
                )
                for c in (0, 128)
            ]
            found.append(jnp.where(low, half[0], half[1]))
        bias[:, pair * 128 : pair * 128 + 128] = jnp.where(left, found[0], found[1])


def start_all(pairs, sems, first=0):
    copies = [pltpu.make_async_copy(a, b, sems.at[first + n]) for n, (a, b) in enumerate(pairs)]
    for copy in copies:
        copy.start()
    return copies


def wait_all(copies):
    for copy in copies:
        copy.wait()


def interior_kernel(
    shifts, tokens_in, grads_in, pad_in, bias_table, rel_index, w_qkv_in, w_out_in,
    updated_out, grad_out, w_part, keys, bias,
    tokens, grads, w_qkv, w_out, marks, updated, tokens_grad,
    xt, xg, hid, istd, qkvg, mix, dq, ones, table, rel, w_sum, sems,
):
    s0, s1 = shifts[0], shifts[1]
    base = lax.axis_index(LON) * 64
    mark_copies = start_all(
        [
            (pad_in.at[pl.ds(pl.multiple_of(base, 8), 64)], marks.at[0:64]),
            (pad_in.at[pl.ds(pl.multiple_of((base + 64) & 1023, 8), 8)], marks.at[64:72]),
        ],
        sems,
    )
    rows_in = start_all([(tokens_in, tokens), (grads_in, grads)], sems, 2)
    weights_in = start_all([(w_qkv_in, w_qkv), (w_out_in, w_out)], sems, 4)
    fill_ones(ones)
    wait_all(mark_copies)
    make_tables(marks, bias_table, rel_index, s0, s1, keys, bias, table, rel)
    wait_all(rows_in)

    def load(a, carry):
        at = pl.ds(s0 + a * WIN, WIN)
        x = pltpu.roll(tokens[at, :, :].astype(F32), 32 - s1, 1)
        g = pltpu.roll(grads[at, :, :].astype(F32), 32 - s1, 1)
        for b in range(3):
            row = pl.multiple_of((a * 3 + b) * CELLS, CELLS)
            c = slice(b * WIN, b * WIN + WIN)
            keep_window(rows_of(x[:, c]), rows_of(g[:, c]), row, xt, xg, hid, istd)
        return carry

    lax.fori_loop(0, 7, load, 0)
    wait_all(weights_in)
    project(21 * CELLS, 448, hid, xg, w_qkv, w_out, qkvg)

    def windows(a, carry):
        seen = [keys[pl.ds(8 * b + a, 1), :] for b in range(3)]
        attend(a * 3, seen, [8] * 3, bias, ones, qkvg, mix, dq)
        return carry

    lax.fori_loop(0, 7, windows, 0)
    copies = []
    for b in range(2):
        r = slice(b * 256, (b + 1) * 256)
        w_sum[r, : 3 * D] = dot_tn(hid[:, r], dq[...])
        w_sum[r, 3 * D :] = dot_tn(mix[:, r], xg[...])
        copies += start_all([(w_sum.at[r], w_part.at[r])], sems, b)

    def store(a, carry):
        at = pl.ds(pl.multiple_of(a * 192, 64), 192)
        to = pl.ds(s0 + a * WIN, WIN)
        for rows, out in zip(finish(at, xt, xg, hid, istd, mix, dq, w_qkv, w_out), (updated, tokens_grad)):
            out[to, :, :] = pltpu.roll(strip_of(rows, 3), s1, 1).astype(BF)
        return carry

    lax.fori_loop(0, 7, store, 0)
    copies += start_all([(updated, updated_out), (tokens_grad, grad_out)], sems, 2)
    wait_all(copies)


def edge_kernel(
    shifts, tokens_in, grads_in, halo_lon, halo_lat, halo_cor, keys, bias, w_qkv_in, w_out_in, w_part,
    lat_up, lon_up, lat_grad, lon_grad, out_lat, out_lon, out_cor, w_mine, w_other,
    tok, grad, far, low_tok, low_grad, low_far, w_qkv, w_out, to_lat, to_lon,
    xt, xg, hid, istd, qkvg, mix, dq, ones, w_sum, sems,
):
    s0, s1 = shifts[0], shifts[1]
    core = lax.axis_index("core")
    thr_edge = jnp.where(lax.axis_index(LAT) == 7, 8 - s1, 8)
    rows_in = start_all(
        [
            (tokens_in.at[:, 16:32, :], tok),
            (grads_in.at[:, 16:32, :], grad),
            (halo_lat, far),
            (tokens_in.at[56:64], low_tok.at[0:8]),
            (grads_in.at[56:64], low_grad.at[0:8]),
            (halo_lon.at[:, :, 0:D], low_tok.at[8:16]),
            (halo_lon.at[:, :, D : 2 * D], low_grad.at[8:16]),
            (halo_lat.at[56:64], low_far.at[0:8]),
            (halo_cor, low_far.at[8:16]),
        ],
        sems,
    )
    weights_in = start_all([(w_qkv_in, w_qkv), (w_out_in, w_out), (w_part, w_sum)], sems, 9)
    fill_ones(ones)
    tail = slice(11 * CELLS, 12 * CELLS)
    xg[tail, :] = jnp.zeros((CELLS, D), BF)
    hid[tail, :] = jnp.zeros((CELLS, D), BF)
    wait_all(rows_in)

    def load(a, carry):
        at = pl.ds(s0 + a * WIN, WIN)
        found = []
        for near, c in ((tok, 0), (grad, D)):
            rows = [near[at, 8:16, :].astype(F32), far[at, :, c : c + D].astype(F32)]
            found.append(rows_of(pltpu.roll(jnp.concatenate(rows, axis=1), 16 - s1, 1)[:, :8]))
        keep_window(*found, pl.multiple_of(a * CELLS, CELLS), xt, xg, hid, istd)
        return carry

    lax.fori_loop(0, 7, load, 0)
    at = pl.ds(s0, WIN)
    found = []
    for near, c in ((low_tok, 0), (low_grad, D)):
        rows = [near[at, :, :].astype(F32), low_far[at, :, c : c + D].astype(F32)]
        found.append(pltpu.roll(jnp.concatenate(rows, axis=1), 40 - s1, 1))
    for b in range(4):
        x, g = (rows_of(rows[:, b * WIN : b * WIN + WIN]) for rows in found)
        keep_window(x, g, (7 + b) * CELLS, xt, xg, hid, istd)
    wait_all(weights_in)
    project(12 * CELLS, 384, hid, xg, w_qkv, w_out, qkvg)

    def windows(a, carry):
        seen, thr = [], []
        for w in range(3):
            n = a * 3 + w
            row = jnp.where(n < 7, 24 + n, jnp.minimum(8 * n - 49, 31))
            seen.append(keys[pl.ds(row, 1), :])
            thr.append(jnp.where((n < 7) | (n == 10), thr_edge, 8))
        attend(a * 3, seen, thr, bias, ones, qkvg, mix, dq)
        return carry

    lax.fori_loop(0, 4, windows, 0)

    results = finish(slice(0, 7 * CELLS), xt, xg, hid, istd, mix, dq, w_qkv, w_out)
    for rows, near, c in zip(results, (tok, grad), (0, D)):
        for a in range(7):
            strip = strip_of(rows[a * CELLS : (a + 1) * CELLS], 1)
            strip = pltpu.roll(strip, s1, 1).astype(BF)
            near[pl.ds(s0 + a * WIN, WIN), 0:8, :] = strip[:, :8]
            to_lat[pl.ds(s0 + a * WIN, WIN), :, c : c + D] = strip[:, 8:]
    results = finish(slice(7 * CELLS, 11 * CELLS), xt, xg, hid, istd, mix, dq, w_qkv, w_out)
    for rows, low, c in zip(results, (low_tok, low_grad), (0, D)):
        strip = pltpu.roll(strip_of(rows, 4), s1, 1).astype(BF)
        low[pl.ds(s0, WIN), :, :] = strip[:, :32]
        to_lat[pl.ds(s0 + 56, WIN), :, c : c + D] = strip[:, 32:]
    to_lon[:, :, 0:D] = low_tok[8:16]
    to_lon[:, :, D : 2 * D] = low_grad[8:16]
    copies = start_all(
        [
            (tok, lat_up),
            (grad, lat_grad),
            (low_tok.at[0:8], lon_up),
            (low_grad.at[0:8], lon_grad),
            (to_lat.at[0:64], out_lat),
            (to_lat.at[64:72], out_cor),
            (to_lon, out_lon),
        ],
        sems,
    )
    for b in range(2):
        r = slice(b * 256, (b + 1) * 256)
        w_sum[r, : 3 * D] += dot_tn(hid[:, r], dq[...])
        w_sum[r, 3 * D :] += dot_tn(mix[:, r], xg[...])

    def split(n, carry):
        to = pl.ds(pl.multiple_of(n * 32, 32), 32)
        w_mine[to, :] = w_sum[pl.ds(pl.multiple_of((2 * n + core) * 32, 32), 32), :].astype(BF)
        w_other[to, :] = w_sum[pl.ds(pl.multiple_of((2 * n + 1 - core) * 32, 32), 32), :].astype(BF)
        return carry

    lax.fori_loop(0, 8, split, 0)
    wait_all(copies)


def edge_merge_kernel(
    shifts, updated, tokens_grad, lat_up, lon_up, lat_grad, lon_grad, out_updated, out_grad,
    side, low, sems,
):
    s0, s1 = shifts[0], shifts[1]
    pairs = []
    for n, out in enumerate((out_updated, out_grad)):
        pairs += [(out.at[:, 16:32, :], side.at[n]), (out.at[56:64, 0:16, :], low.at[n])]
    wait_all(start_all(pairs, sems))
    mark = iota((8, 8, D), 1) >= s1
    for n, (lat, lon) in enumerate(((lat_up, lon_up), (lat_grad, lon_grad))):

        def rest(r, carry, n=n, lat=lat):
            at = pl.ds(pl.multiple_of(r * 8, 8), 8)
            rows = side[n, at, 8:16, :].astype(F32)
            side[n, at, 8:16, :] = jnp.where(mark, lat[at, 0:8, :].astype(F32), rows).astype(BF)
            return carry

        lax.fori_loop(0, 8, rest, 0)
        later = iota((8, 16, D), 0) >= s0
        rows = side[n, 56:64, :, :].astype(F32)
        side[n, 56:64, :, :] = jnp.where(later, lon[:, 16:32, :].astype(F32), rows).astype(BF)
        later = later & (iota((8, 16, D), 1) >= s1)
        rows = low[n].astype(F32)
        low[n] = jnp.where(later, lon[:, 0:16, :].astype(F32), rows).astype(BF)
    wait_all(start_all([(b, a) for a, b in pairs], sems))


def return_kernel(
    shifts, updated, tokens_grad, in_lat, in_lon, in_cor, out_updated, out_grad, side, top, sems
):
    s0, s1 = shifts[0], shifts[1]
    outs = (out_updated, out_grad)
    into = []
    for n, out in enumerate(outs):
        into.append(pltpu.make_async_copy(out.at[:, 0:16, :], side.at[n], sems.at[2 * n]))
        into.append(pltpu.make_async_copy(out.at[0:8, 16:32, :], top.at[n], sems.at[2 * n + 1]))
    for copy in into:
        copy.start()
    for copy in into:
        copy.wait()
    lat = iota((8, 8, D), 1)
    lon = iota((8, 8, D), 0)
    pick = lambda mark, new, old: jnp.where(mark, new.astype(F32), old)
    for n in range(2):
        cols = slice(n * D, n * D + D)

        def rest(r, carry, n=n, cols=cols):
            at = pl.ds(pl.multiple_of(r * 8, 8), 8)
            rows = side[n, at, 0:8, :].astype(F32)
            side[n, at, 0:8, :] = pick(lat < s1, in_lat[at, :, cols], rows).astype(BF)
            return carry

        lax.fori_loop(1, 8, rest, 0)
        rows = side[n, 0:8, 0:8, :].astype(F32)
        rows = pick((lat < s1) & (lon >= s0), in_lat[0:8, :, cols], rows)
        rows = pick((lat >= s1) & (lon < s0), in_lon[:, 0:8, cols], rows)
        rows = pick((lat < s1) & (lon < s0), in_cor[:, :, cols], rows)
        side[n, 0:8, 0:8, :] = rows.astype(BF)
        rows = side[n, 0:8, 8:16, :].astype(F32)
        side[n, 0:8, 8:16, :] = pick(lon < s0, in_lon[:, 8:16, cols], rows).astype(BF)
        rows = top[n].astype(F32)
        top[n] = pick(iota((8, 16, D), 0) < s0, in_lon[:, 16:32, cols], rows).astype(BF)
    back = []
    for n, out in enumerate(outs):
        back.append(pltpu.make_async_copy(side.at[n], out.at[:, 0:16, :], sems.at[2 * n]))
        back.append(pltpu.make_async_copy(top.at[n], out.at[0:8, 16:32, :], sems.at[2 * n + 1]))
    for copy in back:
        copy.start()
    for copy in back:
        copy.wait()


def vmem(shape, dtype):
    return pltpu.VMEM(shape, dtype)


def sds(shape, dtype):
    return jax.ShapeDtypeStruct(shape, dtype)


IN_VMEM = pl.BlockSpec(memory_space=pltpu.VMEM)
IN_SMEM = pl.BlockSpec(memory_space=pltpu.SMEM)
IN_HBM = pl.BlockSpec(memory_space=pl.ANY)


def call(kernel, out_shape, scratch, in_specs, out_specs, aliases=None):
    return pl.pallas_call(
        kernel,
        out_shape=out_shape,
        in_specs=[IN_SMEM] + in_specs,
        out_specs=out_specs,
        scratch_shapes=scratch,
        input_output_aliases=aliases or {},
        compiler_params=pltpu.CompilerParams(vmem_limit_bytes=VMEM_LIMIT),
    )


def window_scratch(rows):
    return [vmem((rows, D), BF), vmem((rows, D), BF), vmem((rows, D), BF), vmem((rows, 128), F32)]


def attend_scratch(rows):
    return [
        vmem((rows, 4 * D), BF),
        vmem((rows, D), BF),
        vmem((rows, 3 * D), BF),
        vmem((GROUP, GROUP), BF),
    ]


def shift_to(value, d_lon, d_lat):
    pairs = []
    for a in range(16):
        for b in range(8):
            pairs.append((a * 8 + b, ((a + d_lon) % 16) * 8 + (b + d_lat) % 8))
    return lax.ppermute(value, ALL, pairs)


def scatter_sum(blocks, axes, count, beside=None):
    here = lax.axis_index(axes)
    parts = [lax.dynamic_index_in_dim(blocks, here, 0, keepdims=False)]
    for step in range(1, count):
        block = lax.dynamic_index_in_dim(blocks, (here + step) % count, 0, keepdims=False)
        pairs = [(n, (n + step) % count) for n in range(count)]
        parts.append(lax.ppermute(block, axes, pairs))
    extra = None
    if beside is not None:
        extra = beside(blocks)
        parts, extra = lax.optimization_barrier((parts, extra))
    total = parts[0].astype(F32)
    for part in parts[1:]:
        total = total + part.astype(F32)
    return total, extra


INNER, OUTER = 21 * CELLS, 12 * CELLS
GRID = sds((64, 32, D), BF)
DMA = pltpu.SemaphoreType.DMA


WEIGHTS = [vmem((D, 3 * D), BF), vmem((D, D), BF)]


def run_interior(*args):
    rows = vmem((64, 32, D), BF)
    return call(
        interior_kernel,
        [GRID, GRID, sds((D, 4 * D), F32), sds((32, 128), F32), sds((64, 512), F32)],
        [rows, rows, *WEIGHTS, vmem((72, 256), jnp.int32), rows, rows]
        + window_scratch(INNER)
        + attend_scratch(INNER)
        + [vmem((8, 256), F32), vmem((64, 128), jnp.int32), vmem((D, 4 * D), F32), DMA((6,))],
        [IN_HBM] * 3 + [IN_VMEM] * 2 + [IN_HBM] * 2,
        [IN_HBM] * 3 + [IN_VMEM] * 2,
    )(*args)


def run_edge(*args):
    lat, lon = (64, 16, D), (8, 32, D)
    far_lat, far_lon = (64, 8, 2 * D), (8, 32, 2 * D)
    return call(
        edge_kernel,
        [sds(shape, BF) for shape in (lat, lon, lat, lon, far_lat, far_lon, (8, 8, 2 * D))]
        + [sds((D // 2, 4 * D), BF)] * 2,
        [vmem(lat, BF), vmem(lat, BF), vmem(far_lat, BF)]
        + [vmem((16, 32, D), BF), vmem((16, 32, D), BF), vmem((16, 8, 2 * D), BF)]
        + WEIGHTS
        + [vmem((72, 8, 2 * D), BF), vmem(far_lon, BF)]
        + window_scratch(OUTER)
        + attend_scratch(OUTER)
        + [vmem((D, 4 * D), F32), DMA((12,))],
        [IN_HBM] * 5 + [IN_VMEM] * 2 + [IN_HBM] * 3,
        [IN_HBM] * 7 + [IN_VMEM] * 2,
    )(*args)


def run_edge_merge(*args):
    return call(
        edge_merge_kernel,
        [GRID, GRID],
        [vmem((2, 64, 16, D), BF), vmem((2, 8, 16, D), BF), DMA((4,))],
        [IN_HBM] * 2 + [IN_VMEM] * 4,
        [IN_HBM] * 2,
        {1: 0, 2: 1},
    )(*args)


def run_return(*args):
    return call(
        return_kernel,
        [GRID, GRID],
        [vmem((2, 64, 16, D), BF), vmem((2, 8, 16, D), BF), DMA((4,))],
        [IN_HBM] * 2 + [IN_VMEM] * 3,
        [IN_HBM] * 2,
        {1: 0, 2: 1},
    )(*args)


def local(tokens, pad_mask, shifts, bias_table, rel_index, w_qkv, w_out, grad_out):
    both = lambda a, b: jnp.concatenate([tokens[a, b], grad_out[a, b]], axis=-1)
    halo_lat = shift_to(both(slice(None), slice(0, 8)), 0, -1)
    halo_lon = shift_to(both(slice(0, 8), slice(None)), -1, 0)
    halo_cor = shift_to(both(slice(0, 8), slice(0, 8)), -1, -1)

    updated, tokens_grad, w_part, keys, bias = run_interior(
        shifts, tokens, grad_out, pad_mask, bias_table, rel_index, w_qkv, w_out
    )
    *edges, out_lat, out_lon, out_cor, w_mine, w_other = run_edge(
        shifts, tokens, grad_out, halo_lon, halo_lat, halo_cor, keys, bias, w_qkv, w_out, w_part
    )

    def merge_beside(blocks):
        _, *placed = lax.optimization_barrier((blocks, updated, tokens_grad))
        return run_edge_merge(shifts, *placed, *edges)

    w_got = lax.ppermute(w_other, "core", [(0, 1), (1, 0)])
    in_lat = shift_to(out_lat, 0, 1)
    in_lon = shift_to(out_lon, 1, 0)
    in_cor = shift_to(out_cor, 1, 1)
    total = (w_mine.astype(F32) + w_got.astype(F32)).astype(BF)
    total = total.reshape(2, 4, 32, 4 * D).transpose(1, 0, 2, 3)
    total, (updated, tokens_grad) = scatter_sum(total, "x", 4, merge_beside)
    total = total.astype(BF).reshape(2, 4, 8, 4 * D).transpose(1, 0, 2, 3)
    total, _ = scatter_sum(total, "y", 4)
    total, _ = scatter_sum(total.astype(BF).reshape(4, 4, 4 * D), ("zh", "zl"), 4)

    updated, tokens_grad = run_return(shifts, updated, tokens_grad, in_lat, in_lon, in_cor)
    return (updated, tokens_grad, total[:, : 3 * D], total[:, 3 * D :])


def solution(mesh):
    fine = Mesh(mesh.devices.reshape(2, 4, 2, 4, 2), ALL)
    in_specs = (P(LON, LAT, None), P(), P(), P(), P(), P(), P(), P(LON, LAT, None))
    out_specs = (P(LON, LAT, None), P(LON, LAT, None), P(ALL, None), P(ALL, None))
    return jax.shard_map(local, mesh=fine, in_specs=in_specs, out_specs=out_specs, check_vma=False)
```

time: 113 us -> 116 us (1.027)
  waiting for transfers between devices: 3.56 us -> 13.9 us
  Pallas kernels: 69.1 us -> 58.8 us
  starting transfers between devices: 28.1 us -> 34.1 us
  local copies, waits for them, and re-layouts: 8.42 us -> 5.55 us
    ppermute x9, waiting for transfers between devices: 0.02 us -> 11.1 us  [scatter_sum(): parts.append(lax.ppermute(block, axes, pairs))]
    pallas_call x5 -> x4, Pallas kernels: 69.1 us -> 58.8 us  [the longest x1 30.7 us: run_interior(): call(interior_kernel, [GRID, GRID, sds((D, 4 * D), F32), sds((32, 128), F...]
    ppermute x9, starting transfers between devices: 13.9 us -> 22.5 us  [scatter_sum(): parts.append(lax.ppermute(block, axes, pairs))]
    ppermute x6, waiting for transfers between devices: 3.53 us -> 0.02 us  [shift_to(): return lax.ppermute(value, ALL, pairs)]
    squeeze x2 -> x0, local copies, waits for them, and re-layouts: 2.88 us -> none  [the longest x1 1.86 us: updated_beside(): edge_lon[0]]
    ppermute x1, waiting for transfers between devices: 0.01 us -> 2.81 us  [local(): w_got = lax.ppermute(w_other, 'core', [(0, 1), (1, 0)])]
    ppermute x6, starting transfers between devices: 14.1 us -> 11.4 us  [shift_to(): return lax.ppermute(value, ALL, pairs)]
    unnamed x22 -> x20, local copies, waits for them, and re-layouts: 2.96 us -> 2.97 us
  transfers between devices with their start and end apart: 16 -> 16, of which waited for: 1 -> 6; matrix products, arithmetic and copies ran while one was open for 4% -> 0% of each run, Pallas kernels for 44% -> 35%
where the time goes in v3:
time: 116 us; the launch traced here: 115 us
  Pallas kernels  58.8 us (51%)
  starting transfers between devices  34.1 us (29%)
  waiting for transfers between devices  13.9 us (12%)
  local copies, waits for them, and re-layouts  5.55 us (5%)
  other arithmetic  2.01 us (2%)
    pallas_call x1, Pallas kernels, run_interior(): call(interior_kernel, [GRID, GRID, sds((D, 4 * D), F32), sds((32, 128), F...  30.7 us
    ppermute x9, starting transfers between devices, scatter_sum(): parts.append(lax.ppermute(block, axes, pairs))  22.5 us
    pallas_call x1, Pallas kernels, run_edge(): call(edge_kernel, [sds(shape, BF) for shape in (lat, lon, lat, lon, far_l...  18.2 us
    ppermute x6, starting transfers between devices, shift_to(): return lax.ppermute(value, ALL, pairs)  11.4 us
    ppermute x9, waiting for transfers between devices, scatter_sum(): parts.append(lax.ppermute(block, axes, pairs))  11.1 us
    pallas_call x1, Pallas kernels, run_edge_merge(): call(edge_merge_kernel, [GRID, GRID], [vmem((2, 64, 16, D), BF), vmem((2,...  5.12 us
    pallas_call x1, Pallas kernels, run_return(): call(return_kernel, [GRID, GRID], [vmem((2, 64, 16, D), BF), vmem((2, 8,...  4.79 us
    unnamed x20, local copies, waits for them, and re-layouts  2.97 us
  transfers between devices with their start and end apart: 16, of which 6 were waited for; matrix products, arithmetic and copies ran while one was open for 0% of the time, Pallas kernels for 35%

profile of v3, /device:TPU:0, one launch (start us, length us, event | category | flops | bytes accessed | tf_op | source)
XLA Modules:
  0.0 115.4 jit_solution(6459231377138915502)
XLA Ops:
  0.7 1.0 slice-done.2
  2.0 4.5 %collective-permute-start.1 = (bf16[64,8,1024]{2,1,0:T(8,128)(2,1)S(1)}, bf16[64,8,1024]{2,1,0:T(8,128)(2,1)S(1)}, u32[]{:S(2)}, u32[]{:S(2)}) collective-permute-start(bf16[64,8,1024]{2,1,0:T(8,128)(2,1)S(1)} %pad_maximum_fusion), channel_id=1, source_target_pairs={{0,7},{1,0},{2,1},{3,2},{4,3},{5,4},{6,5},{7,6},{8,15},{9,8},{10,9... | collective-permute-start | bytes 3145736 | tf_op jit(solution)/shard_map/ppermute | solution.py:462
  6.6 5.0 %collective-permute-start = (bf16[8,32,1024]{2,1,0:T(8,128)(2,1)S(1)}, bf16[8,32,1024]{2,1,0:T(8,128)(2,1)S(1)}, u32[]{:S(2)}, u32[]{:S(2)}) collective-permute-start(bf16[8,32,1024]{2,1,0:T(8,128)(2,1)S(1)} %pad_maximum_fusion.1), channel_id=1, source_target_pairs={{0,120},{1,121},{2,122},{3,123},{4,124},{5,125},{6,126},{7,127},{8... | collective-permute-start | bytes 1572872 | tf_op jit(solution)/shard_map/ppermute | solution.py:462
  11.6 0.3 collective-permute-start.2
  11.9 30.7 %shard_map.111 = (bf16[64,32,512]{2,1,0:T(8,128)(2,1)}, bf16[64,32,512]{2,1,0:T(8,128)(2,1)}, f32[512,2048]{1,0:T(8,128)}, f32[32,128]{1,0:T(8,128)}, f32[64,512]{1,0:T(8,128)}) custom-call(s32[2]{0:T(128)} %shifts.7, bf16[64,32,512]{2,1,0:T(8,128)(2,1)} %tokens_in.3, bf16[64,32,512]{2,1,0:T(8,128)(2,1)} %grads_in.3, s32[1024,256]{1,0:T(8,128)} %pad_in.1, ...), custom_call_target="tpu_custom_call" | custom-call | tf_op jit(solution)/shard_map/pallas_call | solution.py:492
  42.7 0.6 copy-done.6
  43.3 0.2 copy-done.5
  43.5 0.4 copy-done.2
  43.9 18.2 %shard_map.112 = (bf16[64,16,512]{2,1,0:T(8,128)(2,1)}, bf16[8,32,512]{2,1,0:T(8,128)(2,1)}, bf16[64,16,512]{2,1,0:T(8,128)(2,1)}, bf16[8,32,512]{2,1,0:T(8,128)...) custom-call(s32[2]{0:T(128)} %shifts.7, ...), custom_call_target="tpu_custom_call" | custom-call | tf_op jit(solution)/shard_map/pallas_call | solution.py:507
  62.1 0.3 collective-permute-start.3
  62.4 2.8 %collective-permute-done.3 = bf16[256,2048]{1,0:T(8,128)(2,1)S(1)} collective-permute-done((bf16[256,2048]{1,0:T(8,128)(2,1)}, bf16[256,2048]{1,0:T(8,128)(2,1)S(1)}, u32[]{:S(2)}, u32[]{:S(2)}) %collective-permute-start.3) | collective-permute-done | bytes 1048608 | tf_op jit(solution)/shard_map/ppermute | solution.py:562
  65.2 1.6 %add_convert_fusion = bf16[256,2048]{1,0:T(8,128)(2,1)S(1)} fusion(bf16[256,2048]{1,0:T(8,128)(2,1)S(1)} %collective-permute-done.3, bf16[256,2048]{1,0:T(8,128)(2,1)} %get-tuple-element.33), kind=kLoop, calls=%fused_computation | loop fusion | flops 2097152 | bytes 3145728 | tf_op jit(solution)/shard_map/convert_element_type | solution.py:566
  67.0 0.2 collective-permute-start.5
  67.2 3.0 %collective-permute-start.6 = (bf16[2,32,2048]{2,1,0:T(8,128)(2,1)S(1)}, bf16[2,32,2048]{2,1,0:T(8,128)(2,1)S(1)}, u32[]{:S(2)}, u32[]{:S(2)}) collective-permute-start(bf16[2,32,2048]{2,1,0:T(8,128)(2,1)S(1)} %get-tuple-element.56), channel_id=1, source_target_pairs={{0,48},{16,0},{32,16},{48,32},{1,49},{17,1},{33,17},{49,33},{2,50}... | collective-permute-start | bytes 786440 | tf_op jit(solution)/shard_map/ppermute | solution.py:471
  70.2 1.6 %collective-permute-start.7 = (bf16[64,8,1024]{2,1,0:T(8,128)(2,1)}, bf16[64,8,1024]{2,1,0:T(8,128)(2,1)S(1)}, u32[]{:S(2)}, u32[]{:S(2)}) collective-permute-start(bf16[64,8,1024]{2,1,0:T(8,128)(2,1)} %get-tuple-element.47), channel_id=1, source_target_pairs={{0,1},{1,2},{2,3},{3,4},{4,5},{5,6},{6,7},{7,0},{8,9},{9,10},{10,1... | collective-permute-start | bytes 3145736 | tf_op jit(solution)/shard_map/ppermute | solution.py:462
  71.8 5.1 %shard_map.113 = (bf16[64,32,512]{2,1,0:T(8,128)(2,1)}, bf16[64,32,512]{2,1,0:T(8,128)(2,1)}) custom-call(s32[2]{0:T(128)} %shifts.7, bf16[64,32,512]{2,1,0:T(8,128)(2,1)} %get-tuple-element.37.updated, bf16[64,32,512]{2,1,0:T(8,128)(2,1)} %get-tuple-element.38.tokens_grad, ...), custom_call_target="tpu_custom_call", output_to_operand_aliasing={{0}: (1, {}), {1}: (2, {})} | custom-call | tf_op jit(solution)/shard_map/pallas_call | solution.py:524
  76.9 5.2 %collective-permute-done.4 = bf16[2,32,2048]{2,1,0:T(8,128)(2,1)S(1)} collective-permute-done((bf16[2,32,2048]{2,1,0:T(8,128)(2,1)S(1)}, bf16[2,32,2048]{2,1,0:T(8,128)(2,1)S(1)}, u32[]{:S(2)}, u32[]{:S(2)}) %collective-permute-start.4) | collective-permute-done | bytes 262176 | tf_op jit(solution)/shard_map/ppermute | solution.py:471
  82.2 0.6 collective-permute-done.6
  83.0 0.8 collective-permute-start.12
  83.8 0.3 collective-permute-start.11
  84.1 1.0 collective-permute-start.10
  85.1 2.2 %collective-permute-done.12 = bf16[2,8,2048]{2,1,0:T(8,128)(2,1)S(1)} collective-permute-done((bf16[2,8,2048]{2,1,0:T(8,128)(2,1)S(1)}, bf16[2,8,2048]{2,1,0:T(8,128)(2,1)S(1)}, u32[]{:S(2)}, u32[]{:S(2)}) %collective-permute-start.12) | collective-permute-done | bytes 65568 | tf_op jit(solution)/shard_map/ppermute | solution.py:471
  87.3 2.4 %collective-permute-done.11 = bf16[2,8,2048]{2,1,0:T(8,128)(2,1)S(1)} collective-permute-done((bf16[2,8,2048]{2,1,0:T(8,128)(2,1)S(1)}, bf16[2,8,2048]{2,1,0:T(8,128)(2,1)S(1)}, u32[]{:S(2)}, u32[]{:S(2)}) %collective-permute-start.11) | collective-permute-done | bytes 65568 | tf_op jit(solution)/shard_map/ppermute | solution.py:471
  89.7 0.7 collective-permute-done.10
  90.4 11.5 %collective-permute-start.15 = (bf16[4,2048]{1,0:T(4,128)(2,1)S(1)}, bf16[4,2048]{1,0:T(4,128)(2,1)S(1)}, u32[]{:S(2)}, u32[]{:S(2)}) collective-permute-start(bf16[4,2048]{1,0:T(4,128)(2,1)S(1)} %get-tuple-element.64), channel_id=1, source_target_pairs={{0,65},{1,0},{64,1},{65,64},{2,67},{3,2},{66,3},{67,66},{4,69},{5,... | collective-permute-start | bytes 49160 | tf_op jit(solution)/shard_map/ppermute | solution.py:471
  101.9 5.6 %collective-permute-start.14 = (bf16[4,2048]{1,0:T(4,128)(2,1)S(1)}, bf16[4,2048]{1,0:T(4,128)(2,1)S(1)}, u32[]{:S(2)}, u32[]{:S(2)}) collective-permute-start(bf16[4,2048]{1,0:T(4,128)(2,1)S(1)} %get-tuple-element.65), channel_id=1, source_target_pairs={{0,64},{1,65},{64,0},{65,1},{2,66},{3,67},{66,2},{67,3},{4,68},{5,... | collective-permute-start | bytes 49160 | tf_op jit(solution)/shard_map/ppermute | solution.py:471
  107.5 0.6 copy-done.7
  108.1 0.2 copy-done.4
  108.3 1.0 copy-done.3
  109.3 4.8 %shard_map.114 = (bf16[64,32,512]{2,1,0:T(8,128)(2,1)}, bf16[64,32,512]{2,1,0:T(8,128)(2,1)}) custom-call(s32[2]{0:T(128)} %shifts.7, bf16[64,32,512]{2,1,0:T(8,128)(2,1)} %get-tuple-element.45.updated, bf16[64,32,512]{2,1,0:T(8,128)(2,1)} %get-tuple-element.46.tokens_grad, ...), custom_call_target="tpu_custom_call", output_to_operand_aliasing={{0}: (1, {}), {1}: (2, {})} | custom-call | tf_op jit(solution)/shard_map/pallas_call | solution.py:535
  114.2 0.6 slice.32
  114.8 0.6 slice.33
  (47 shorter events, 0.9 us)
Async XLA Ops:
  0.6 1.0 slice-start.2
  0.6 1.2 %slice-start = ((bf16[64,32,512]{2,1,0:T(8,128)(2,1)}), bf16[64,8,512]{2,1,0:T(8,128)(2,1)S(1)}, s32[]{:S(2)}) async-start(bf16[64,32,512]{2,1,0:T(8,128)(2,1)} %tokens_in.3), calls=%async_computation | async-start | bytes 1048576 | tf_op jit(solution)/shard_map/slice | solution.py:546
  0.7 5.9 %slice-start.1 = ((bf16[64,32,512]{2,1,0:T(8,128)(2,1)}), bf16[8,32,512]{2,1,0:T(8,128)(2,1)S(1)}, s32[]{:S(2)}) async-start(bf16[64,32,512]{2,1,0:T(8,128)(2,1)} %tokens_in.3), calls=%async_computation.1 | async-start | bytes 524288 | tf_op jit(solution)/shard_map/slice | solution.py:546
  0.7 5.8 %slice-start.3 = ((bf16[64,32,512]{2,1,0:T(8,128)(2,1)}), bf16[8,32,512]{2,1,0:T(8,128)(2,1)S(1)}, s32[]{:S(2)}) async-start(bf16[64,32,512]{2,1,0:T(8,128)(2,1)} %grads_in.3), calls=%async_computation.3 | async-start | bytes 524288 | tf_op jit(solution)/shard_map/slice | solution.py:546
  0.7 10.9 %copy-start.1 = (bf16[64,32,512]{2,1,0:T(8,128)(2,1)S(1)}, bf16[64,32,512]{2,1,0:T(8,128)(2,1)}, u32[]{:S(2)}) copy-start(bf16[64,32,512]{2,1,0:T(8,128)(2,1)} %grads_in.3) | copy-start | bytes 6291460
  1.8 9.8 %copy-start = (bf16[64,32,512]{2,1,0:T(8,128)(2,1)S(1)}, bf16[64,32,512]{2,1,0:T(8,128)(2,1)}, u32[]{:S(2)}) copy-start(bf16[64,32,512]{2,1,0:T(8,128)(2,1)} %tokens_in.3) | copy-start | bytes 6291460
  2.0 40.7 %collective-permute-start.1 = (bf16[64,8,1024]{2,1,0:T(8,128)(2,1)S(1)}, bf16[64,8,1024]{2,1,0:T(8,128)(2,1)S(1)}, u32[]{:S(2)}, u32[]{:S(2)}) collective-permute-start(bf16[64,8,1024]{2,1,0:T(8,128)(2,1)S(1)} %pad_maximum_fusion), channel_id=1, source_target_pairs={{0,7},{1,0},{2,1},{3,2},{4,3},{5,4},{6,5},{7,6},{8,15},{9,8},{10,9... | collective-permute-start | bytes 3145736 | tf_op jit(solution)/shard_map/ppermute | solution.py:462
  6.6 36.1 %collective-permute-start = (bf16[8,32,1024]{2,1,0:T(8,128)(2,1)S(1)}, bf16[8,32,1024]{2,1,0:T(8,128)(2,1)S(1)}, u32[]{:S(2)}, u32[]{:S(2)}) collective-permute-start(bf16[8,32,1024]{2,1,0:T(8,128)(2,1)S(1)} %pad_maximum_fusion.1), channel_id=1, source_target_pairs={{0,120},{1,121},{2,122},{3,123},{4,124},{5,125},{6,126},{7,127},{8... | collective-permute-start | bytes 1572872 | tf_op jit(solution)/shard_map/ppermute | solution.py:462
  11.6 31.0 %collective-permute-start.2 = (bf16[8,8,1024]{2,1,0:T(8,128)(2,1)S(1)}, bf16[8,8,1024]{2,1,0:T(8,128)(2,1)S(1)}, u32[]{:S(2)}, u32[]{:S(2)}) collective-permute-start(bf16[8,8,1024]{2,1,0:T(8,128)(2,1)S(1)} %pad_maximum_fusion.2), channel_id=1, source_target_pairs={{0,127},{1,120},{2,121},{3,122},{4,123},{5,124},{6,125},{7,126},{8... | collective-permute-start | bytes 393224 | tf_op jit(solution)/shard_map/ppermute | solution.py:462
  42.6 0.7 copy-start.6
  42.7 0.8 copy-start.5
  42.7 1.2 %copy-start.2 = (bf16[64,8,1024]{2,1,0:T(8,128)(2,1)}, bf16[64,8,1024]{2,1,0:T(8,128)(2,1)S(1)}, u32[]{:S(2)}) copy-start(bf16[64,8,1024]{2,1,0:T(8,128)(2,1)S(1)} %collective-permute-done.1.halo_lat) | copy-start | bytes 3145732
  62.1 3.1 %collective-permute-start.3 = (bf16[256,2048]{1,0:T(8,128)(2,1)}, bf16[256,2048]{1,0:T(8,128)(2,1)S(1)}, u32[]{:S(2)}, u32[]{:S(2)}) collective-permute-start(bf16[256,2048]{1,0:T(8,128)(2,1)} %get-tuple-element.34), channel_id=1, source_target_pairs={{0,8},{8,0},{1,9},{9,1},{2,10},{10,2},{3,11},{11,3},{4,12},{12,4},... | collective-permute-start | bytes 3145736 | tf_op jit(solution)/shard_map/ppermute | solution.py:562
  66.9 15.2 %collective-permute-start.4 = (bf16[2,32,2048]{2,1,0:T(8,128)(2,1)S(1)}, bf16[2,32,2048]{2,1,0:T(8,128)(2,1)S(1)}, u32[]{:S(2)}, u32[]{:S(2)}) collective-permute-start(bf16[2,32,2048]{2,1,0:T(8,128)(2,1)S(1)} %get-tuple-element.58), channel_id=1, source_target_pairs={{0,16},{16,32},{32,48},{48,0},{1,17},{17,33},{33,49},{49,1},{2,18}... | collective-permute-start | bytes 786440 | tf_op jit(solution)/shard_map/ppermute | solution.py:471
  67.0 15.2 %collective-permute-start.5 = (bf16[2,32,2048]{2,1,0:T(8,128)(2,1)S(1)}, bf16[2,32,2048]{2,1,0:T(8,128)(2,1)S(1)}, u32[]{:S(2)}, u32[]{:S(2)}) collective-permute-start(bf16[2,32,2048]{2,1,0:T(8,128)(2,1)S(1)} %get-tuple-element.57), channel_id=1, source_target_pairs={{0,32},{16,48},{32,0},{48,16},{1,33},{17,49},{33,1},{49,17},{2,34}... | collective-permute-start | bytes 786440 | tf_op jit(solution)/shard_map/ppermute | solution.py:471
  67.2 15.6 %collective-permute-start.6 = (bf16[2,32,2048]{2,1,0:T(8,128)(2,1)S(1)}, bf16[2,32,2048]{2,1,0:T(8,128)(2,1)S(1)}, u32[]{:S(2)}, u32[]{:S(2)}) collective-permute-start(bf16[2,32,2048]{2,1,0:T(8,128)(2,1)S(1)} %get-tuple-element.56), channel_id=1, source_target_pairs={{0,48},{16,0},{32,16},{48,32},{1,49},{17,1},{33,17},{49,33},{2,50}... | collective-permute-start | bytes 786440 | tf_op jit(solution)/shard_map/ppermute | solution.py:471
  70.2 37.3 %collective-permute-start.7 = (bf16[64,8,1024]{2,1,0:T(8,128)(2,1)}, bf16[64,8,1024]{2,1,0:T(8,128)(2,1)S(1)}, u32[]{:S(2)}, u32[]{:S(2)}) collective-permute-start(bf16[64,8,1024]{2,1,0:T(8,128)(2,1)} %get-tuple-element.47), channel_id=1, source_target_pairs={{0,1},{1,2},{2,3},{3,4},{4,5},{5,6},{6,7},{7,0},{8,9},{9,10},{10,1... | collective-permute-start | bytes 3145736 | tf_op jit(solution)/shard_map/ppermute | solution.py:462
  71.8 13.3 %copy-start.8 = (bf16[8,32,1024]{2,1,0:T(8,128)(2,1)S(1)}, bf16[8,32,1024]{2,1,0:T(8,128)(2,1)}, u32[]{:S(2)}) copy-start(bf16[8,32,1024]{2,1,0:T(8,128)(2,1)} %get-tuple-element.48) | copy-start | bytes 1572868
  71.8 15.5 %copy-start.9 = (bf16[8,8,1024]{2,1,0:T(8,128)(2,1)S(1)}, bf16[8,8,1024]{2,1,0:T(8,128)(2,1)}, u32[]{:S(2)}) copy-start(bf16[8,8,1024]{2,1,0:T(8,128)(2,1)} %get-tuple-element.49) | copy-start | bytes 393220
  83.0 4.3 %collective-permute-start.12 = (bf16[2,8,2048]{2,1,0:T(8,128)(2,1)S(1)}, bf16[2,8,2048]{2,1,0:T(8,128)(2,1)S(1)}, u32[]{:S(2)}, u32[]{:S(2)}) collective-permute-start(bf16[2,8,2048]{2,1,0:T(8,128)(2,1)S(1)} %get-tuple-element.61), channel_id=1, source_target_pairs={{0,6},{2,0},{4,2},{6,4},{1,7},{3,1},{5,3},{7,5},{8,14},{10,8},{12,... | collective-permute-start | bytes 196616 | tf_op jit(solution)/shard_map/ppermute | solution.py:471
  83.8 5.9 %collective-permute-start.11 = (bf16[2,8,2048]{2,1,0:T(8,128)(2,1)S(1)}, bf16[2,8,2048]{2,1,0:T(8,128)(2,1)S(1)}, u32[]{:S(2)}, u32[]{:S(2)}) collective-permute-start(bf16[2,8,2048]{2,1,0:T(8,128)(2,1)S(1)} %get-tuple-element.62), channel_id=1, source_target_pairs={{0,4},{2,6},{4,0},{6,2},{1,5},{3,7},{5,1},{7,3},{8,12},{10,14},{12... | collective-permute-start | bytes 196616 | tf_op jit(solution)/shard_map/ppermute | solution.py:471
  84.1 6.2 %collective-permute-start.10 = (bf16[2,8,2048]{2,1,0:T(8,128)(2,1)S(1)}, bf16[2,8,2048]{2,1,0:T(8,128)(2,1)S(1)}, u32[]{:S(2)}, u32[]{:S(2)}) collective-permute-start(bf16[2,8,2048]{2,1,0:T(8,128)(2,1)S(1)} %get-tuple-element.60), channel_id=1, source_target_pairs={{0,2},{2,4},{4,6},{6,0},{1,3},{3,5},{5,7},{7,1},{8,10},{10,12},{12... | collective-permute-start | bytes 196616 | tf_op jit(solution)/shard_map/ppermute | solution.py:471
  85.1 22.4 %collective-permute-start.8 = (bf16[8,32,1024]{2,1,0:T(8,128)(2,1)S(1)}, bf16[8,32,1024]{2,1,0:T(8,128)(2,1)S(1)}, u32[]{:S(2)}, u32[]{:S(2)}) collective-permute-start(bf16[8,32,1024]{2,1,0:T(8,128)(2,1)S(1)} %copy-done.8), channel_id=1, source_target_pairs={{0,8},{1,9},{2,10},{3,11},{4,12},{5,13},{6,14},{7,15},{8,16},{9,17... | collective-permute-start | bytes 1572872 | tf_op jit(solution)/shard_map/ppermute | solution.py:462
  87.3 20.2 %collective-permute-start.9 = (bf16[8,8,1024]{2,1,0:T(8,128)(2,1)S(1)}, bf16[8,8,1024]{2,1,0:T(8,128)(2,1)S(1)}, u32[]{:S(2)}, u32[]{:S(2)}) collective-permute-start(bf16[8,8,1024]{2,1,0:T(8,128)(2,1)S(1)} %copy-done.9), channel_id=1, source_target_pairs={{0,9},{1,10},{2,11},{3,12},{4,13},{5,14},{6,15},{7,8},{8,17},{9,18... | collective-permute-start | bytes 393224 | tf_op jit(solution)/shard_map/ppermute | solution.py:462
  90.4 23.7 %collective-permute-start.15 = (bf16[4,2048]{1,0:T(4,128)(2,1)S(1)}, bf16[4,2048]{1,0:T(4,128)(2,1)S(1)}, u32[]{:S(2)}, u32[]{:S(2)}) collective-permute-start(bf16[4,2048]{1,0:T(4,128)(2,1)S(1)} %get-tuple-element.64), channel_id=1, source_target_pairs={{0,65},{1,0},{64,1},{65,64},{2,67},{3,2},{66,3},{67,66},{4,69},{5,... | collective-permute-start | bytes 49160 | tf_op jit(solution)/shard_map/ppermute | solution.py:471
  101.9 12.2 %collective-permute-start.14 = (bf16[4,2048]{1,0:T(4,128)(2,1)S(1)}, bf16[4,2048]{1,0:T(4,128)(2,1)S(1)}, u32[]{:S(2)}, u32[]{:S(2)}) collective-permute-start(bf16[4,2048]{1,0:T(4,128)(2,1)S(1)} %get-tuple-element.65), channel_id=1, source_target_pairs={{0,64},{1,65},{64,0},{65,1},{2,66},{3,67},{66,2},{67,3},{4,68},{5,... | collective-permute-start | bytes 49160 | tf_op jit(solution)/shard_map/ppermute | solution.py:471
  107.5 0.7 copy-start.7
  107.5 6.6 %collective-permute-start.13 = (bf16[4,2048]{1,0:T(4,128)(2,1)S(1)}, bf16[4,2048]{1,0:T(4,128)(2,1)S(1)}, u32[]{:S(2)}, u32[]{:S(2)}) collective-permute-start(bf16[4,2048]{1,0:T(4,128)(2,1)S(1)} %get-tuple-element.63), channel_id=1, source_target_pairs={{0,1},{1,64},{64,65},{65,0},{2,3},{3,66},{66,67},{67,2},{4,5},{5,6... | collective-permute-start | bytes 49160 | tf_op jit(solution)/shard_map/ppermute | solution.py:471
  107.5 0.8 copy-start.4
  108.3 1.0 copy-start.3
